TPU v7x, 32 devices: a whole 2x2x4 slice. The times are simulated.
32 devices in a mesh: dp: 4 (over y, x), fsdp: 8 (over z, core).
Axes of the slice: x: 2, y: 2, z: 4, core: 2. Of those that a mesh axis runs over, the one named last changes fastest.
Arguments:
- gradient: bfloat16 [4, 4096, 2, 1024], P('dp', 'fsdp'), may hold values from -3 to 3
- block_owner_index: int32 [8], replicated, may hold values from 0 to 7, as said below
- block_grid_cell: int32 [8], replicated, may hold values from 0 to 7, each once
- left_eigen_basis: float32 [16, 1024, 1024], P('fsdp', None, 'dp'), may hold values from -0.1875 to 0.1875
- right_eigen_basis: float32 [16, 1024, 1024], P('fsdp', None, 'dp'), may hold values from -0.1875 to 0.1875
- left_statistic_matrix: float32 [16, 1024, 1024], P('fsdp', None, 'dp'), may hold values from -6 to 6
- right_statistic_matrix: float32 [16, 1024, 1024], P('fsdp', None, 'dp'), may hold values from -6 to 6
- first_adam_moment: float32 [16, 1024, 1024], P('fsdp', None, 'dp'), may hold values from -0.09 to 0.09
- second_adam_moment: float32 [16, 1024, 1024], P('fsdp', None, 'dp'), may hold values from 1e-05 to 0.001
Outputs:
- new_left_stat: float32 [16, 1024, 1024], P('fsdp', None, 'dp')
- new_right_stat: float32 [16, 1024, 1024], P('fsdp', None, 'dp')
- new_first: float32 [16, 1024, 1024], P('fsdp', None, 'dp')
- new_second: float32 [16, 1024, 1024], P('fsdp', None, 'dp')
- update: bfloat16 [4096, 2, 1024], P('fsdp', None, 'dp')
Inputs may be any that keep to these rules, and one draw needn't show every extreme that they name: `block_owner_index`: no fsdp index owns more than 2 blocks; a quarter of the fsdp indices own 2 blocks and a quarter own none.
All inputs are finite; a program needn't handle non-finite values.
Results may differ from a plain program's by a relative error of at most 0.013.
Values may be sent and summed in bfloat16 or wider, within the bound.
A program may use at most 128 MiB of HBM per device.

v0:
```python
import jax
import jax.numpy as jnp
from jax import lax
from jax.sharding import PartitionSpec as P


def slot_lookup_table(block_owner_index, block_grid_cell, slot_count, per_owner):
    block_ids = jnp.arange(block_owner_index.shape[0], dtype=jnp.int32)
    shared = (block_owner_index[:, None] == block_owner_index[None, :]) & (
        block_ids[None, :] < block_ids[:, None]
    )
    rank_in = jnp.sum(shared.astype(jnp.int32), axis=1)
    block_slot_index = block_owner_index * per_owner + rank_in
    slot_ids = jnp.arange(slot_count, dtype=jnp.int32)
    matches = (block_slot_index[None, :] == slot_ids[:, None]).astype(jnp.int32)
    filled_marker = jnp.sum(matches, axis=1)
    slot_grid_cell = jnp.sum(matches * block_grid_cell[None, :], axis=1)
    return (block_slot_index, filled_marker, slot_grid_cell)


def local(
    gradient,
    block_owner_index,
    block_grid_cell,
    left_eigen_basis,
    right_eigen_basis,
    left_statistic_matrix,
    right_statistic_matrix,
    first_adam_moment,
    second_adam_moment,
):
    highest = lax.Precision.HIGHEST
    replicas = lax.axis_size("dp")
    members = lax.axis_size("fsdp")
    member = lax.axis_index("fsdp")
    column_group = lax.axis_index("dp")
    per_owner = left_eigen_basis.shape[0]
    block = left_eigen_basis.shape[1]
    width = left_eigen_basis.shape[2]
    band_rows = gradient.shape[1]
    grid_cols = gradient.shape[2]
    bands = block // band_rows
    grid_rows = members // bands
    piece_rows = band_rows // members
    slot_count = per_owner * members
    partial_terms = gradient.reshape(band_rows, grid_cols, replicas, width).astype(jnp.float32)
    reduced = lax.psum_scatter(
        partial_terms.astype(jnp.bfloat16), "dp", scatter_dimension=2, tiled=True
    ).astype(jnp.float32)
    reduced = reduced.reshape(band_rows, grid_cols, width).astype(jnp.bfloat16)
    block_slot_index, filled_marker, slot_grid_cell = slot_lookup_table(
        block_owner_index, block_grid_cell, slot_count, per_owner
    )
    my_filled = lax.dynamic_slice_in_dim(filled_marker, member * per_owner, per_owner, 0)
    split_band = reduced.reshape(members, piece_rows, grid_cols, width)
    received = lax.all_to_all(split_band, "fsdp", split_axis=0, concat_axis=0, tiled=True)
    by_cell = received.reshape(grid_rows, bands, piece_rows, grid_cols, width)
    by_cell = jnp.transpose(by_cell, (0, 3, 1, 2, 4)).reshape(
        grid_rows * grid_cols, bands, piece_rows, width
    )
    leaving = jnp.take(by_cell, slot_grid_cell, axis=0)
    leaving = jnp.where((filled_marker > 0)[:, None, None, None], leaving, jnp.zeros_like(leaving))
    leaving = leaving.reshape(members, per_owner, bands, piece_rows, width)
    landed = lax.all_to_all(leaving, "fsdp", split_axis=0, concat_axis=0, tiled=True)
    col_piece = jnp.transpose(landed, (1, 2, 0, 3, 4)).reshape(per_owner, block, width)
    gathered = lax.all_gather(col_piece, "dp", axis=2, tiled=True)
    row_piece = lax.dynamic_slice_in_dim(gathered, column_group * width, width, 1)
    new_left = 0.95 * left_statistic_matrix + 0.05 * jnp.einsum(
        "sik,sjk->sij", gathered, row_piece, preferred_element_type=jnp.float32
    )
    new_right = 0.95 * right_statistic_matrix + 0.05 * jnp.einsum(
        "ski,skj->sij", gathered, col_piece, preferred_element_type=jnp.float32
    )
    half_turn = jnp.einsum(
        "sik,sij->skj", left_eigen_basis, gathered.astype(jnp.float32), precision=highest
    ).astype(jnp.bfloat16)
    turned = jnp.einsum(
        "skj,sjc->skc",
        lax.all_gather(half_turn, "dp", axis=1, tiled=True).astype(jnp.float32),
        right_eigen_basis,
        precision=highest,
    )
    new_first = 0.9 * first_adam_moment + 0.1 * turned
    new_second = 0.999 * second_adam_moment + 0.001 * turned * turned
    direction = new_first / (jnp.sqrt(new_second) + 1e-08)
    flipped = jnp.transpose(direction, (1, 0, 2))
    piece = flipped
    mixed = lax.psum_scatter(
        jnp.einsum("isc,sjc->isj", piece, right_eigen_basis, precision=highest),
        "dp",
        scatter_dimension=0,
        tiled=True,
    )
    piece = mixed
    moved = lax.psum_scatter(
        jnp.einsum("ksj,sik->jsi", piece, left_eigen_basis, precision=highest),
        "dp",
        scatter_dimension=0,
        tiled=True,
    )
    backward = jnp.transpose(moved.astype(jnp.bfloat16), (1, 2, 0))
    parted = backward.reshape(per_owner, bands, members, piece_rows, width)
    parted = jnp.transpose(parted, (2, 0, 1, 3, 4))
    parted = jnp.where((my_filled > 0)[None, :, None, None, None], parted, jnp.zeros_like(parted))
    homed = lax.all_to_all(parted, "fsdp", split_axis=0, concat_axis=0, tiled=True)
    homed = homed.reshape(slot_count, bands, piece_rows, width)
    all_cells = jnp.arange(grid_rows * grid_cols, dtype=jnp.int32)
    all_hits = (block_grid_cell[None, :] == all_cells[:, None]).astype(jnp.int32)
    cell_slot = jnp.sum(all_hits * block_slot_index[None, :], axis=1)
    per_cell = jnp.take(homed, cell_slot, axis=0).reshape(
        grid_rows, grid_cols, bands, piece_rows, width
    )
    per_cell = jnp.transpose(per_cell, (0, 2, 3, 1, 4)).reshape(
        members, piece_rows, grid_cols, width
    )
    update = lax.all_to_all(per_cell, "fsdp", split_axis=0, concat_axis=0, tiled=True).reshape(
        band_rows, grid_cols, width
    )
    return (new_left, new_right, new_first, new_second, update)


def solution(mesh):
    in_specs = (
        P("dp", "fsdp", None, None),
        P(),
        P(),
        P("fsdp", None, "dp"),
        P("fsdp", None, "dp"),
        P("fsdp", None, "dp"),
        P("fsdp", None, "dp"),
        P("fsdp", None, "dp"),
        P("fsdp", None, "dp"),
    )
    out_specs = (
        P("fsdp", None, "dp"),
        P("fsdp", None, "dp"),
        P("fsdp", None, "dp"),
        P("fsdp", None, "dp"),
        P("fsdp", None, "dp"),
    )
    return jax.shard_map(local, mesh=mesh, in_specs=in_specs, out_specs=out_specs, check_vma=False)
```

profile of v0, /device:TPU:0, one launch (start us, length us, event | category | flops | bytes accessed | tf_op | source)
XLA Modules:
  0.0 525.5 jit_solution(1089309147820697659)
XLA Ops:
  7.2 0.0 copy-start
  7.2 0.0 all-reduce.3.cloned.1.call-start
  7.2 6.3 %copy.73 = bf16[1,512,2,1024]{1,3,2,0:T(8,128)(2,1)} copy(bf16[1,512,2,1024]{3,2,1,0:T(2,128)(2,1)} %param.9) | data formatting | bytes 4194304 | tf_op args[0]
  13.5 0.0 all-reduce.3.cloned.1.call-update
  13.5 0.6 copy-done.10
  14.2 0.6 dynamic-slice
  14.8 0.0 copy-done.9
  14.8 0.2 convert_reduce_fusion.1
  14.9 71.1 %all-reduce.3.cloned.1.call-done = bf16[512,2,4,256]{0,3,2,1:T(8,128)(2,1)} async-done(((bf16[512,2,4,256]{0,3,2,1:T(8,128)(2,1)}), bf16[512,2,4,256]{0,3,2,1:T(8,128)(2,1)}) %all-reduce.3.cloned.1.call-update) | async-done | bytes 2097168
  86.0 1.7 constant_dynamic-slice_fusion
  87.8 0.2 copy.74
  88.0 0.8 copy.75
  88.8 4.6 all-to-all-start
  93.4 0.0 all-gather.3.cloned.1.call-start
  93.5 0.0 copy-done.8
  93.5 0.1 convert_reduce_fusion
  93.6 0.1 reduce_sum.47
  93.7 0.1 gt.14
  93.8 15.0 %all-to-all-done = bf16[8,64,2,256]{3,1,2,0:T(8,128)(2,1)S(1)} async-done(((bf16[8,64,2,256]{3,1,2,0:T(8,128)(2,1)}), bf16[8,64,2,256]{3,1,2,0:T(8,128)(2,1)S(1)}, u32[]{:S(2)}, u32[]{:S(2)}) %all-to-all-start) | async-done | bytes 524320 | tf_op jit(solution)/shard_map/all_to_all | solution.py:56
  108.8 1.6 gather_fusion
  110.4 1.4 select_select_fusion
  111.9 29.0 %all_to_all.20 = bf16[8,2,2,64,256]{4,3,2,1,0:T(8,128)(2,1)S(1)} all-to-all(bf16[8,2,2,64,256]{4,3,2,1,0:T(8,128)(2,1)S(1)} %select_select_fusion), channel_id=1, replica_groups=mesh['dp'=4,'fsdp'=8] {'fsdp'}, dimensions={0} | all-to-all | bytes 2097152 | tf_op jit(solution)/shard_map/all_to_all | solution.py:64
  140.9 1.0 copy.77
  141.9 0.0 all-gather.3.cloned.1.call-update
  141.9 0.0 all-gather.5.cloned.1.call-start
  142.0 50.6 %all-gather.3.cloned.1.call-done = bf16[2,1024,1024]{2,1,0:T(8,128)(2,1)} async-done(((bf16[2,1024,256]{2,1,0:T(8,128)(2,1)}), bf16[2,1024,1024]{2,1,0:T(8,128)(2,1)}) %all-gather.3.cloned.1.call-update) | async-done | bytes 4194320 | tf_op jit(solution)/shard_map/all_gather | solution.py:66
  192.6 8.0 %fusion.5 = bf16[2,256,1024]{1,2,0:T(8,128)(2,1)} fusion(bf16[2,1024,1024]{2,1,0:T(8,128)(2,1)} %all-gather.3.cloned.1.call-done, f32[2,1024,256]{2,1,0:T(8,128)} %param.12), kind=kOutput, calls=%fused_computation.14 | convolution fusion | flops 6442975232 | bytes 7340032 | tf_op jit(solution)/shard_map/sik,sij->skj/dot_general | solution.py:74
  200.6 0.0 all-gather.5.cloned.1.call-update
  200.6 0.2 reduce-scatter.6.cloned.1.call-start
  200.9 52.5 %all-gather.5.cloned.1.call-done = bf16[2,1024,1024]{1,2,0:T(8,128)(2,1)} async-done(((bf16[2,256,1024]{1,2,0:T(8,128)(2,1)}), bf16[2,1024,1024]{1,2,0:T(8,128)(2,1)}) %all-gather.5.cloned.1.call-update) | async-done | bytes 4194320 | tf_op jit(solution)/shard_map/all_gather | solution.py:79
  253.3 0.0 copy-done
  253.4 7.9 %fusion = (f32[2,1024,256]{2,1,0:T(8,128)S(1)}, f32[2,1024,256]{2,1,0:T(8,128)S(1)}) fusion(f32[2,1024,256]{2,1,0:T(8,128)} %param.17, f32[2,1024,256]{2,1,0:T(8,128)} %param.16, bf16[2,1024,1024]{1,2,0:T(8,128)(2,1)} %all-gather.5.cloned.1.call-done, f32[2,1024,256]{2,1,0:T(8,128)S(1)} %copy-done), kind=kOutput, calls=%fused_computation.5 | convolution fusion | flops 6446120960 | bytes 14680064 | tf_op jit(solution)/shard_map/skj,sjc->skc/dot_general | solution.py:77
  261.2 0.0 copy-start.4
  261.2 0.0 copy-start.5
  261.2 1.3 copy-done.4
  262.5 0.7 copy-done.5
  263.2 9.6 %convolution_bitcast_fusion.1 = f32[1024,2,1024]{2,0,1:T(8,128)} fusion(f32[2,1024,256]{2,1,0:T(8,128)S(1)} %copy-done, f32[2,1024,256]{2,1,0:T(8,128)S(1)} %get-tuple-element.28, f32[2,1024,256]{2,1,0:T(8,128)S(1)} %get-tuple-element.27), kind=kOutput, calls=%fused_computation.3 | convolution fusion | flops 6443499520 | bytes 14680064 | tf_op jit(solution)/shard_map/isc,sjc->isj/dot_general | solution.py:89
  272.8 0.0 reduce-scatter.6.cloned.1.call-update
  272.8 0.3 reduce-scatter.8.cloned.1.call-start
  273.1 86.3 %reduce-scatter.6.cloned.1.call-done = f32[256,2,1024]{2,0,1:T(8,128)} async-done(((f32[1024,2,1024]{2,0,1:T(8,128)}), f32[256,2,1024]{2,0,1:T(8,128)}) %reduce-scatter.6.cloned.1.call-update) | async-done | bytes 2097168 | tf_op jit(solution)/shard_map/reduce_scatter | solution.py:88
  359.4 0.0 copy-done.6
  359.4 16.6 %convolution_bitcast_fusion = f32[1024,2,1024]{2,0,1:T(8,128)} fusion(f32[256,2,1024]{2,0,1:T(8,128)} %reduce-scatter.6.cloned.1.call-done, f32[2,1024,256]{2,1,0:T(8,128)S(1)} %copy-done.6), kind=kOutput, calls=%fused_computation.2 | convolution fusion | flops 6442450944 | bytes 12582912 | tf_op jit(solution)/shard_map/ksj,sik->jsi/dot_general | solution.py:96
  376.0 0.0 reduce-scatter.8.cloned.1.call-update
  376.1 0.1 dynamic-slice_compare_fusion
  376.1 86.4 %reduce-scatter.8.cloned.1.call-done = f32[256,2,1024]{2,0,1:T(8,128)} async-done(((f32[1024,2,1024]{2,0,1:T(8,128)}), f32[256,2,1024]{2,0,1:T(8,128)}) %reduce-scatter.8.cloned.1.call-update) | async-done | bytes 2097168 | tf_op jit(solution)/shard_map/reduce_scatter | solution.py:95
  462.6 1.7 convert_bitcast_fusion
  464.3 0.5 copy.82
  464.9 0.1 select_bitcast_fusion
  465.0 1.1 copy.83
  466.1 4.6 all-to-all-start.2
  470.7 0.1 select_reduce_fusion
  470.8 0.1 reduce_sum.50
  470.9 26.4 %all-to-all-done.2 = bf16[8,2,2,64,256]{4,3,2,1,0:T(8,128)(2,1)S(1)} async-done(((bf16[8,2,2,64,256]{4,3,2,1,0:T(8,128)(2,1)}), bf16[8,2,2,64,256]{4,3,2,1,0:T(8,128)(2,1)S(1)}, u32[]{:S(2)}, u32[]{:S(2)}) %all-to-all-start.2) | async-done | bytes 1048608 | tf_op jit(solution)/shard_map/all_to_all | solution.py:105
  497.3 0.6 gather_fusion.1
  497.9 0.1 select_bitcast_fusion.1
  498.0 0.8 copy.84
  498.8 3.5 all-to-all-start.3
  502.3 0.0 copy-start.3
  502.4 0.0 copy-start.7
  502.4 6.0 %multiply_add_fusion.2 = f32[2,1024,256]{2,1,0:T(8,128)} fusion(f32[2,1024,256]{2,1,0:T(8,128)} %param.14, bf16[2,1024,1024]{2,1,0:T(8,128)(2,1)} %all-gather.3.cloned.1.call-done, s32[]{:T(128)S(6)} %select_n.66), kind=kOutput, calls=%fused_computation.12 | convolution fusion | flops 1075314688 | bytes 9437188 | tf_op jit(solution)/shard_map/sik,sjk->sij/dot_general | solution.py:68
  508.4 0.0 copy-start.1
  508.4 3.1 multiply_add_fusion.1
  511.5 6.1 %all-to-all-done.3 = bf16[8,64,2,256]{3,1,2,0:T(8,128)(2,1)S(1)} async-done(((bf16[8,64,2,256]{3,1,2,0:T(8,128)(2,1)}), bf16[8,64,2,256]{3,1,2,0:T(8,128)(2,1)S(1)}, u32[]{:S(2)}, u32[]{:S(2)}) %all-to-all-start.3) | async-done | bytes 524320 | tf_op jit(solution)/shard_map/all_to_all | solution.py:116
  517.7 1.3 copy.86
  (19 shorter events, 0.1 us)
Async XLA Ops:
  7.2 246.2 %copy-start = (f32[2,1024,256]{2,1,0:T(8,128)S(1)}, f32[2,1024,256]{2,1,0:T(8,128)}, u32[]{:S(2)}) copy-start(f32[2,1024,256]{2,1,0:T(8,128)} %param.13) | copy-start | bytes 6291460
  7.2 78.9 %all-reduce.3.cloned.1.call-start = ((), (), s32[]{:S(2)}) async-start(), calls=%async_computation.10 | async-start | bytes 4194304
  13.5 0.7 copy-start.10
  13.5 1.2 copy-start.9
  86.0 7.4 %copy-start.8 = (s32[8]{0:T(128)S(1)}, s32[8]{0:T(128)}, u32[]{:S(2)}) copy-start(s32[8]{0:T(128)} %param.11) | copy-start | bytes 100
  88.8 20.0 %all-to-all-start = ((bf16[8,64,2,256]{3,1,2,0:T(8,128)(2,1)}), bf16[8,64,2,256]{3,1,2,0:T(8,128)(2,1)S(1)}, u32[]{:S(2)}, u32[]{:S(2)}) async-start(bf16[8,64,2,256]{3,1,2,0:T(8,128)(2,1)} %copy.75), calls=%async_computation | async-start | bytes 1048576 | tf_op jit(solution)/shard_map/all_to_all | solution.py:56
  93.4 99.2 %all-gather.3.cloned.1.call-start = ((), (), s32[]{:S(2)}) async-start(), calls=%async_computation.6 | async-start | bytes 5242880 | tf_op jit(solution)/shard_map/all_gather | solution.py:66
  141.9 111.4 %all-gather.5.cloned.1.call-start = ((), (), s32[]{:S(2)}) async-start(), calls=%async_computation.7 | async-start | bytes 5242880 | tf_op jit(solution)/shard_map/all_gather | solution.py:79
  200.6 158.8 %reduce-scatter.6.cloned.1.call-start = ((), (), s32[]{:S(2)}) async-start(), calls=%async_computation.8 | async-start | bytes 10485760 | tf_op jit(solution)/shard_map/reduce_scatter | solution.py:88
  261.2 1.3 copy-start.4
  261.2 2.0 copy-start.5
  272.8 86.6 %copy-start.6 = (f32[2,1024,256]{2,1,0:T(8,128)S(1)}, f32[2,1024,256]{2,1,0:T(8,128)}, u32[]{:S(2)}) copy-start(f32[2,1024,256]{2,1,0:T(8,128)} %param.12) | copy-start | bytes 6291460
  272.8 189.7 %reduce-scatter.8.cloned.1.call-start = ((), (), s32[]{:S(2)}) async-start(), calls=%async_computation.9 | async-start | bytes 10485760 | tf_op jit(solution)/shard_map/reduce_scatter | solution.py:95
  466.1 31.2 %all-to-all-start.2 = ((bf16[8,2,2,64,256]{4,3,2,1,0:T(8,128)(2,1)}), bf16[8,2,2,64,256]{4,3,2,1,0:T(8,128)(2,1)S(1)}, u32[]{:S(2)}, u32[]{:S(2)}) async-start(bf16[8,2,2,64,256]{4,3,2,1,0:T(8,128)(2,1)} %copy.83), calls=%async_computation.4 | async-start | bytes 2097152 | tf_op jit(solution)/shard_map/all_to_all | solution.py:105
  498.8 18.8 %all-to-all-start.3 = ((bf16[8,64,2,256]{3,1,2,0:T(8,128)(2,1)}), bf16[8,64,2,256]{3,1,2,0:T(8,128)(2,1)S(1)}, u32[]{:S(2)}, u32[]{:S(2)}) async-start(bf16[8,64,2,256]{3,1,2,0:T(8,128)(2,1)} %bitcast.22), calls=%async_computation.5 | async-start | bytes 1048576 | tf_op jit(solution)/shard_map/all_to_all | solution.py:116
  502.3 6.0 %copy-start.2 = (bf16[2,1024,1024]{2,1,0:T(8,128)(2,1)S(1)}, bf16[2,1024,1024]{2,1,0:T(8,128)(2,1)}, u32[]{:S(2)}) copy-start(bf16[2,1024,1024]{2,1,0:T(8,128)(2,1)} %all-gather.3.cloned.1.call-done) | copy-start | bytes 12582916
  502.3 6.0 %copy-start.3 = (bf16[2,2,8,64,256]{4,3,2,1,0:T(8,128)(2,1)S(1)}, bf16[2,2,8,64,256]{4,3,2,1,0:T(8,128)(2,1)}, u32[]{:S(2)}) copy-start(bf16[2,2,8,64,256]{4,3,2,1,0:T(8,128)(2,1)} %copy.77) | copy-start | bytes 3145732
  502.4 6.0 %copy-start.7 = (f32[2,1024,256]{2,1,0:T(8,128)S(1)}, f32[2,1024,256]{2,1,0:T(8,128)}, u32[]{:S(2)}) copy-start(f32[2,1024,256]{2,1,0:T(8,128)} %param.15) | copy-start | bytes 6291460
  508.4 10.6 %copy-start.1 = (f32[2,1024,256]{2,1,0:T(8,128)S(1)}, f32[2,1024,256]{2,1,0:T(8,128)}, u32[]{:S(2)}) copy-start(f32[2,1024,256]{2,1,0:T(8,128)} %param.13) | copy-start | bytes 6291460
Sparse Core Ops, SparseCore 0:
  13.7 72.3 all-reduce.2
  142.1 50.4 all-gather.2
  200.7 52.5 all-gather.4
  273.0 86.4 reduce-scatter.5
  376.2 86.3 reduce-scatter.7
where the time goes:
time: 526 us
  waiting for transfers between devices  394 us (75%)
  matrix products  51.2 us (10%)
  blocking collectives  29 us (6%)
  local copies, waits for them, and re-layouts  19.6 us (4%)
  between operations  14 us (3%)
  starting transfers between devices  13.3 us (3%)
    reduce_scatter x1, waiting for transfers between devices, local(): lax.psum_scatter(jnp.einsum('ksj,sik->jsi', piece, left_eigen_basis, prec...  86.4 us
    reduce_scatter x1, waiting for transfers between devices, local(): lax.psum_scatter(jnp.einsum('isc,sjc->isj', piece, right_eigen_basis, pre...  86.3 us
    unnamed x6, waiting for transfers between devices  71.2 us
    all_gather x1, waiting for transfers between devices, local(): lax.all_gather(half_turn, 'dp', axis=1, tiled=True).astype(jnp.float32)  52.5 us
    all_gather x1, waiting for transfers between devices, local(): gathered = lax.all_gather(col_piece, 'dp', axis=2, tiled=True)  50.6 us
    all_to_all x1, blocking collectives, local(): lax.all_to_all(leaving, 'fsdp', split_axis=0, concat_axis=0, tiled=True)  29 us
    all_to_all x1, waiting for transfers between devices, local(): lax.all_to_all(parted, 'fsdp', split_axis=0, concat_axis=0, tiled=True)  26.4 us
    dot_general x1, matrix products, local(): jnp.einsum('ksj,sik->jsi', piece, left_eigen_basis, precision=highest)  16.6 us
  transfers between devices with their start and end apart: 8, of which 8 were waited for; matrix products, arithmetic and copies ran while one was open for 2% of the time, Pallas kernels for 0%

commit v1 on v0

v1 whole, which is shorter than its diff:
```python
import jax
import jax.numpy as jnp
from jax import lax
from jax.sharding import PartitionSpec as P


def slot_lookup_table(block_owner_index, block_grid_cell, slot_count, per_owner):
    block_ids = jnp.arange(block_owner_index.shape[0], dtype=jnp.int32)
    shared = (block_owner_index[:, None] == block_owner_index[None, :]) & (
        block_ids[None, :] < block_ids[:, None]
    )
    rank_in = jnp.sum(shared.astype(jnp.int32), axis=1)
    block_slot_index = block_owner_index * per_owner + rank_in
    slot_ids = jnp.arange(slot_count, dtype=jnp.int32)
    matches = (block_slot_index[None, :] == slot_ids[:, None]).astype(jnp.int32)
    filled_marker = jnp.sum(matches, axis=1)
    slot_grid_cell = jnp.sum(matches * block_grid_cell[None, :], axis=1)
    return (filled_marker, slot_grid_cell)


def local(
    gradient,
    block_owner_index,
    block_grid_cell,
    left_eigen_basis,
    right_eigen_basis,
    left_statistic_matrix,
    right_statistic_matrix,
    first_adam_moment,
    second_adam_moment,
):
    bf16, f32 = jnp.bfloat16, jnp.float32
    replicas = lax.axis_size("dp")
    members = lax.axis_size("fsdp")
    member = lax.axis_index("fsdp")
    column_group = lax.axis_index("dp")
    per_owner, block, width = left_eigen_basis.shape
    band_rows, grid_cols = gradient.shape[1:3]
    bands = block // band_rows
    grid_rows = members // bands
    cells = grid_rows * grid_cols

    filled_marker, slot_grid_cell = slot_lookup_table(
        block_owner_index, block_grid_cell, per_owner * members, per_owner
    )
    my_filled = lax.dynamic_slice_in_dim(filled_marker, member * per_owner, per_owner, 0)
    my_cell = lax.dynamic_slice_in_dim(slot_grid_cell, member * per_owner, per_owner, 0)

    left = left_eigen_basis.astype(bf16)
    right = right_eigen_basis.astype(bf16)
    left_full = lax.all_gather(left, "dp", axis=2, tiled=True)

    terms = jnp.transpose(
        gradient.reshape(band_rows, grid_cols, replicas, width), (2, 1, 0, 3)
    ).reshape(replicas * grid_cols * band_rows, width)
    reduced = lax.psum_scatter(terms, "dp", scatter_dimension=0, tiled=True)
    everyone = lax.all_gather(reduced, "fsdp", axis=0, tiled=True)
    everyone = everyone.reshape(grid_rows, bands, grid_cols, band_rows, width)
    pieces = []
    for k in range(per_owner):
        cell = my_cell[k]
        piece = lax.dynamic_slice(
            everyone,
            (cell // grid_cols, 0, cell % grid_cols, 0, 0),
            (1, bands, 1, band_rows, width),
        ).reshape(block, width)
        pieces.append(jnp.where(my_filled[k] > 0, piece, jnp.zeros_like(piece)))
    col_piece = jnp.stack(pieces)
    gathered = lax.all_gather(col_piece, "dp", axis=2, tiled=True)
    row_piece = lax.dynamic_slice_in_dim(gathered, column_group * width, width, 1)

    turned_right = jnp.einsum(
        "skj,sjc->skc", gathered, right, preferred_element_type=f32
    ).astype(bf16)
    turned = jnp.einsum("ski,skc->sic", left_full, turned_right, preferred_element_type=f32)
    new_first = 0.9 * first_adam_moment + 0.1 * turned
    new_second = 0.999 * second_adam_moment + 0.001 * turned * turned
    direction = (new_first / (jnp.sqrt(new_second) + 1e-08)).astype(bf16)
    mixed = jnp.einsum("sik,skc->sic", left_full, direction, preferred_element_type=f32).astype(bf16)
    partial = jnp.einsum(
        "sic,sdjc->dsij",
        mixed,
        right.reshape(per_owner, replicas, width, width),
        preferred_element_type=f32,
    ).astype(bf16)
    back = lax.psum_scatter(
        partial.reshape(replicas * per_owner * block, width), "dp", scatter_dimension=0, tiled=True
    ).reshape(per_owner, bands, band_rows, width)

    new_left = 0.95 * left_statistic_matrix + 0.05 * jnp.einsum(
        "sik,sjk->sij", gathered, row_piece, preferred_element_type=f32
    )
    new_right = 0.95 * right_statistic_matrix + 0.05 * jnp.einsum(
        "ski,skj->sij", gathered, col_piece, preferred_element_type=f32
    )

    placed = []
    for cell in range(cells):
        here = jnp.zeros((bands, band_rows, width), bf16)
        for k in range(per_owner):
            here = jnp.where((my_filled[k] > 0) & (my_cell[k] == cell), back[k], here)
        placed.append(here)
    placed = jnp.stack(placed).reshape(grid_rows, grid_cols, bands, band_rows, width)
    placed = jnp.transpose(placed, (0, 2, 1, 3, 4)).reshape(members * grid_cols * band_rows, width)
    mine = lax.psum_scatter(placed, "fsdp", scatter_dimension=0, tiled=True)
    update = jnp.transpose(mine.reshape(grid_cols, band_rows, width), (1, 0, 2))
    return (new_left, new_right, new_first, new_second, update)


def solution(mesh):
    slots = P("fsdp", None, "dp")
    in_specs = (P("dp", "fsdp", None, None), P(), P()) + (slots,) * 6
    return jax.shard_map(
        local, mesh=mesh, in_specs=in_specs, out_specs=(slots,) * 5, check_vma=False
    )
```

time: 526 us -> 348 us (0.66)
  waiting for transfers between devices: 394 us -> 256 us
  blocking collectives: 29 us -> 0 us
  matrix products: 51.2 us -> 25.9 us
  between operations: 14 us -> 30.9 us
  starting transfers between devices: 13.3 us -> 0.42 us
  local copies, waits for them, and re-layouts: 19.6 us -> 28.1 us
    unnamed x6, waiting for transfers between devices: 71.2 us -> 0.1 us
    reduce_scatter x2 -> x3, waiting for transfers between devices: 173 us -> 117 us  [the longest x1 42.5 us: local(): lax.psum_scatter(partial.reshape(replicas * per_owner * block, width), 'd...]
    all_to_all x3 -> x0, waiting for transfers between devices: 47.4 us -> none  [the longest x1 26.4 us: local(): lax.all_to_all(parted, 'fsdp', split_axis=0, concat_axis=0, tiled=True)]
    all_gather x1 -> x2, waiting for transfers between devices: 52.5 us -> 84.2 us  [the longest x1 44.6 us: local(): left_full = lax.all_gather(left, 'dp', axis=2, tiled=True)]
    all_to_all x1 -> x0, blocking collectives: 29 us -> none  [local(): lax.all_to_all(leaving, 'fsdp', split_axis=0, concat_axis=0, tiled=True)]
    dot_general x6 -> x4, matrix products: 51.2 us -> 25.9 us  [the longest x1 9 us: local(): jnp.einsum('ski,skc->sic', left_full, turned_right, preferred_element_typ...]
    all_to_all x3 -> x0, starting transfers between devices: 12.7 us -> none  [the longest x1 4.61 us: local(): lax.all_to_all(split_band, 'fsdp', split_axis=0, concat_axis=0, tiled=True)]
    unnamed x26 -> x29, local copies, waits for them, and re-layouts: 12.6 us -> 17.7 us
  transfers between devices with their start and end apart: 8 -> 6, of which waited for: 8 -> 6; matrix products, arithmetic and copies ran while one was open for 2% -> 7% of each run, Pallas kernels for 0% -> 0%
where the time goes in v1:
time: 348 us
  waiting for transfers between devices  256 us (74%)
  between operations  30.9 us (9%)
  local copies, waits for them, and re-layouts  28.1 us (8%)
  matrix products  25.9 us (7%)
  other arithmetic  6.4 us (2%)
    all_gather x1, waiting for transfers between devices, local(): gathered = lax.all_gather(col_piece, 'dp', axis=2, tiled=True)  55 us
    all_gather x1, waiting for transfers between devices, local(): left_full = lax.all_gather(left, 'dp', axis=2, tiled=True)  44.6 us
    reduce_scatter x1, waiting for transfers between devices, local(): lax.psum_scatter(partial.reshape(replicas * per_owner * block, width), 'd...  42.5 us
    all_gather x1, waiting for transfers between devices, local(): everyone = lax.all_gather(reduced, 'fsdp', axis=0, tiled=True)  39.5 us
    reduce_scatter x1, waiting for transfers between devices, local(): reduced = lax.psum_scatter(terms, 'dp', scatter_dimension=0, tiled=True)  38 us
    reduce_scatter x1, waiting for transfers between devices, local(): mine = lax.psum_scatter(placed, 'fsdp', scatter_dimension=0, tiled=True)  36.3 us
    unnamed x29, local copies, waits for them, and re-layouts  17.7 us
    dot_general x1, matrix products, local(): jnp.einsum('ski,skc->sic', left_full, turned_right, preferred_element_typ...  9 us
  transfers between devices with their start and end apart: 6, of which 6 were waited for; matrix products, arithmetic and copies ran while one was open for 7% of the time, Pallas kernels for 0%

profile of v1, /device:TPU:0, one launch (start us, length us, event | category | flops | bytes accessed | tf_op | source)
XLA Modules:
  0.0 347.8 jit_solution(3609230524628949907)
XLA Ops:
  7.2 0.0 reduce-scatter.4.cloned.1.call-start
  7.2 4.7 %copy.38 = bf16[1,512,2,1024]{1,3,2,0:T(8,128)(2,1)S(1)} copy(bf16[1,512,2,1024]{3,2,1,0:T(2,128)(2,1)} %param.9) | data formatting | bytes 4194304 | tf_op args[0]
  11.9 2.3 copy.39
  14.3 0.0 copy-start.2
  14.3 0.0 reduce-scatter.4.cloned.1.call-update
  14.3 0.0 all-gather.4.cloned.1.call-start
  14.4 38.0 %reduce-scatter.4.cloned.1.call-done = bf16[1024,256]{1,0:T(8,128)(2,1)} async-done(((bf16[4096,256]{1,0:T(8,128)(2,1)}), bf16[1024,256]{1,0:T(8,128)(2,1)}) %reduce-scatter.4.cloned.1.call-update) | async-done | bytes 524304 | tf_op jit(solution)/shard_map/reduce_scatter | solution.py:56
  52.4 0.0 all-gather.4.cloned.1.call-update
  52.4 0.0 copy-start.7
  52.4 0.0 copy-start.5
  52.4 0.0 all-gather.8.cloned.1.call-start
  52.4 0.0 copy-done.2
  52.5 1.1 convert_element_type.32
  53.5 0.0 all-gather.8.cloned.1.call-update
  53.6 0.0 all-gather.6.cloned.1.call-start
  53.6 0.0 copy-done.7
  53.6 0.2 convert_reduce_fusion.1
  53.8 0.0 copy-done.5
  53.8 0.1 convert_reduce_fusion
  53.9 0.1 dynamic_slice.16
  54.0 0.6 fusion.12
  59.7 0.1 dynamic_slice.15
  59.8 0.6 fusion.11
  61.7 39.5 %all-gather.4.cloned.1.call-done = bf16[8192,256]{1,0:T(8,128)(2,1)} async-done(((bf16[1024,256]{1,0:T(8,128)(2,1)}), bf16[8192,256]{1,0:T(8,128)(2,1)}) %all-gather.4.cloned.1.call-update) | async-done | bytes 4194320 | tf_op jit(solution)/shard_map/all_gather | solution.py:57
  101.2 1.3 dynamic-slice_select_fusion.1
  102.5 0.0 copy-start.3
  102.5 1.1 pad_maximum_fusion
  103.6 0.0 all-gather.6.cloned.1.call-update
  103.6 0.0 reduce-scatter.6.cloned.1.call-start
  103.7 0.8 copy-done.3
  104.5 1.1 convert_element_type.30
  105.6 0.0 copy-start.4
  105.6 3.0 copy.41
  108.7 0.0 copy-done.4
  108.7 1.8 copy.43
  110.5 44.6 %all-gather.8.cloned.1.call-done = bf16[2,1024,1024]{2,1,0:T(8,128)(2,1)} async-done(((bf16[2,1024,256]{2,1,0:T(8,128)(2,1)}), bf16[2,1024,1024]{2,1,0:T(8,128)(2,1)}) %all-gather.8.cloned.1.call-update) | async-done | bytes 4194320 | tf_op jit(solution)/shard_map/all_gather | solution.py:51
  155.1 55.0 %all-gather.6.cloned.1.call-done = bf16[2,1024,1024]{2,1,0:T(8,128)(2,1)} async-done(((bf16[2,1024,256]{2,1,0:T(8,128)(2,1)}), bf16[2,1024,1024]{2,1,0:T(8,128)(2,1)}) %all-gather.6.cloned.1.call-update) | async-done | bytes 4194320 | tf_op jit(solution)/shard_map/all_gather | solution.py:69
  210.1 9.0 %fusion = (f32[2,1024,256]{1,2,0:T(8,128)}, f32[2,1024,256]{1,2,0:T(8,128)S(1)}) fusion(f32[2,1024,256]{1,2,0:T(8,128)} %copy.43, f32[2,1024,256]{1,2,0:T(8,128)} %copy.41, bf16[2,1024,1024]{2,1,0:T(8,128)(2,1)} %all-gather.8.cloned.1.call-done, bf16[2,1024,1024]{2,1,0:T(8,128)(2,1)} %all-gather.6.cloned.1.call-done, ...), kind=kOutput, calls=%fused_computation.2 | convolution fusion | flops 2151677952 | bytes 17825792 | tf_op jit(solution)/shard_map/ski,skc->sic/dot_general | solution.py:75
  219.1 7.7 %convert_bitcast_fusion = bf16[4,2,1024,256]{3,2,0,1:T(8,128)(2,1)} fusion(bf16[2,4,256,256]{3,2,1,0:T(8,128)(2,1)} %bitcast.57, bf16[2,1024,1024]{2,1,0:T(8,128)(2,1)} %all-gather.8.cloned.1.call-done, f32[2,1024,256]{1,2,0:T(8,128)S(1)} %get-tuple-element.30, f32[2,1024,256]{1,2,0:T(8,128)} %get-tuple-element.29), kind=kOutput, calls=%fused_computation | convolution fusion | flops 2151677952 | bytes 13631488 | tf_op jit(solution)/shard_map/sic,sdjc->dsij/dot_general | solution.py:80
  226.8 4.4 %copy.45 = bf16[4,2,1024,256]{3,2,1,0:T(8,128)(2,1)} copy(bf16[4,2,1024,256]{3,2,0,1:T(8,128)(2,1)} %convert_bitcast_fusion) | data formatting | bytes 8388608 | tf_op jit(solution)/shard_map/convert_element_type | solution.py:85
  231.3 0.0 reduce-scatter.6.cloned.1.call-update
  231.3 0.2 reduce-scatter.8.cloned.1.call-start
  241.7 42.5 %reduce-scatter.6.cloned.1.call-done = bf16[2048,256]{1,0:T(8,128)(2,1)} async-done(((bf16[8192,256]{1,0:T(8,128)(2,1)}), bf16[2048,256]{1,0:T(8,128)(2,1)}) %reduce-scatter.6.cloned.1.call-update) | async-done | bytes 1048592 | tf_op jit(solution)/shard_map/reduce_scatter | solution.py:86
  284.2 0.0 copy-start.1
  284.2 1.4 select_select_fusion.1
  285.7 0.0 copy-done.1
  285.7 0.1 select_select_fusion
  286.1 2.3 copy.46
  288.4 0.0 reduce-scatter.8.cloned.1.call-update
  288.4 2.9 copy.48
  291.3 1.8 copy.47
  293.1 0.0 copy-start
  293.1 0.0 copy-start.6
  293.1 6.5 %multiply_add_fusion = f32[2,1024,256]{2,1,0:T(8,128)} fusion(f32[2,1024,256]{2,1,0:T(8,128)} %param.15, bf16[2,1024,1024]{2,1,0:T(8,128)(2,1)} %all-gather.6.cloned.1.call-done, bf16[1,1024,256]{2,1,0:T(8,128)(2,1)S(1)} %bitcast.56, bf16[1,1024,256]{2,1,0:T(8,128)(2,1)S(1)} %bitcast.54), kind=kOutput, calls=%fused_computation.6 | convolution fusion | flops 1075838976 | bytes 9437184 | tf_op jit(solution)/shard_map/ski,skj->sij/dot_general | solution.py:93
  299.6 0.0 copy-done
  299.6 0.0 copy-done.6
  299.6 2.7 multiply_add_fusion.1
  302.3 36.3 %reduce-scatter.8.cloned.1.call-done = bf16[1024,256]{1,0:T(8,128)(2,1)} async-done(((bf16[8192,256]{1,0:T(8,128)(2,1)}), bf16[1024,256]{1,0:T(8,128)(2,1)}) %reduce-scatter.8.cloned.1.call-update) | async-done | bytes 524304 | tf_op jit(solution)/shard_map/reduce_scatter | solution.py:105
  338.6 2.4 copy.49
  (9 shorter events, 0.3 us)
Async XLA Ops:
  7.2 45.2 %reduce-scatter.4.cloned.1.call-start = ((), (), s32[]{:S(2)}) async-start(), calls=%async_computation.3 | async-start | bytes 2621440 | tf_op jit(solution)/shard_map/reduce_scatter | solution.py:56
  14.3 38.2 %copy-start.2 = (f32[2,1024,256]{2,1,0:T(8,128)S(1)}, f32[2,1024,256]{2,1,0:T(8,128)}, u32[]{:S(2)}) copy-start(f32[2,1024,256]{2,1,0:T(8,128)} %param.12) | copy-start | bytes 6291460
  14.3 86.9 %all-gather.4.cloned.1.call-start = ((), (), s32[]{:S(2)}) async-start(), calls=%async_computation.4 | async-start | bytes 4718592 | tf_op jit(solution)/shard_map/all_gather | solution.py:57
  52.4 1.2 copy-start.7
  52.4 1.4 copy-start.5
  52.4 102.7 %all-gather.8.cloned.1.call-start = ((), (), s32[]{:S(2)}) async-start(), calls=%async_computation.6 | async-start | bytes 5242880 | tf_op jit(solution)/shard_map/all_gather | solution.py:51
  53.6 156.5 %all-gather.6.cloned.1.call-start = ((), (), s32[]{:S(2)}) async-start(), calls=%async_computation.5 | async-start | bytes 5242880 | tf_op jit(solution)/shard_map/all_gather | solution.py:69
  102.5 2.0 copy-start.3
  103.6 180.6 %reduce-scatter.6.cloned.1.call-start = ((), (), s32[]{:S(2)}) async-start(), calls=%async_computation.7 | async-start | bytes 5242880 | tf_op jit(solution)/shard_map/reduce_scatter | solution.py:86
  105.6 3.0 copy-start.4
  231.3 107.3 %reduce-scatter.8.cloned.1.call-start = ((), (), s32[]{:S(2)}) async-start(), calls=%async_computation.8 | async-start | bytes 4718592 | tf_op jit(solution)/shard_map/reduce_scatter | solution.py:105
  284.2 1.5 copy-start.1
  293.1 6.5 %copy-start = (bf16[2,1024,1024]{2,1,0:T(8,128)(2,1)S(1)}, bf16[2,1024,1024]{2,1,0:T(8,128)(2,1)}, u32[]{:S(2)}) copy-start(bf16[2,1024,1024]{2,1,0:T(8,128)(2,1)} %all-gather.6.cloned.1.call-done) | copy-start | bytes 12582916
  293.1 6.5 %copy-start.6 = (f32[2,1024,256]{2,1,0:T(8,128)S(1)}, f32[2,1024,256]{2,1,0:T(8,128)}, u32[]{:S(2)}) copy-start(f32[2,1024,256]{2,1,0:T(8,128)} %param.14) | copy-start | bytes 6291460
Sparse Core Ops, SparseCore 0:
  14.4 37.8 reduce-scatter.3
  54.0 47.1 all-gather.3
  103.8 51.2 all-gather.7
  157.5 52.5 all-gather.5
  231.4 52.7 reduce-scatter.5
  288.5 50.0 reduce-scatter.7

commit v2 on v1

v2 whole, which is shorter than its diff:
```python
import functools

import jax
import jax.numpy as jnp
from jax import lax
from jax.experimental import pallas as pl
from jax.experimental.pallas import tpu as pltpu
from jax.sharding import PartitionSpec as P

MESH = pl.DeviceIdType.MESH


def meet(replicas, members, d, m):
    barrier = pltpu.get_barrier_semaphore()
    for o in range(1, replicas):
        pl.semaphore_signal(
            barrier, inc=1, device_id={"dp": lax.rem(d + o, replicas)}, device_id_type=MESH
        )
    for o in range(1, members):
        pl.semaphore_signal(
            barrier, inc=1, device_id={"fsdp": lax.rem(m + o, members)}, device_id_type=MESH
        )
    pl.semaphore_wait(barrier, replicas + members - 2)


def push(src, dst, send, recv, axis, to):
    copy = pltpu.make_async_remote_copy(
        src_ref=src,
        dst_ref=dst,
        send_sem=send,
        recv_sem=recv,
        device_id={axis: to},
        device_id_type=MESH,
    )
    copy.start()
    return copy


def spread_first(full, mine, d, sems):
    width = mine.shape[2]
    here = full.at[:, :, pl.ds(pl.multiple_of(d * width, width), width)]
    own = pltpu.make_async_copy(mine, here, sems.at[2, 0])
    own.start()
    one = push(mine, here, sems.at[0, 0], sems.at[1, 0], "dp", d + 1 - 2 * lax.rem(d, 2))
    two = push(mine, here, sems.at[0, 1], sems.at[1, 1], "dp", lax.rem(d + 2, 4))
    return own, one, two


def spread_relay(full, width, d, sems, first):
    half = full.shape[1] // 2
    d1 = d + 1 - 2 * lax.rem(d, 2)
    d2 = lax.rem(d + 2, 4)
    first[1].wait_recv()
    top = full.at[:, pl.ds(0, half), pl.ds(pl.multiple_of(d1 * width, width), width)]
    a = push(top, top, sems.at[0, 2], sems.at[1, 2], "dp", d2)
    first[2].wait_recv()
    low = full.at[:, pl.ds(half, half), pl.ds(pl.multiple_of(d2 * width, width), width)]
    b = push(low, low, sems.at[0, 3], sems.at[1, 3], "dp", d1)
    return a, b


def bring_kernel(
    replicas, members, at_ref, fill_ref, terms, left, gath, leftf, col,
    inbox, red, p1, p2, rs, s1, s2, gs, ls,
):
    d, m = lax.axis_index("dp"), lax.axis_index("fsdp")
    per_owner, block, width = left.shape
    grid_cols, piece = terms.shape[2:4]
    bands = p2.shape[2]
    f32, bf16 = jnp.float32, jnp.bfloat16
    meet(replicas, members, d, m)
    sums = []
    for o in range(1, replicas):
        to = lax.rem(d + o, replicas)
        sums.append(push(terms.at[to], inbox.at[d], rs.at[0, o], rs.at[1, o], "dp", to))
    for c in sums:
        c.wait_recv()
    out = []
    for p in range(members):
        to = lax.rem(m + p, members)
        acc = terms[d, to].astype(f32)
        for o in range(1, replicas):
            acc += inbox[lax.rem(d + o, replicas), to].astype(f32)
        if p:
            red[to] = acc.astype(bf16)
            out.append(
                push(
                    red.at[to], p1.at[pl.ds(m * grid_cols, grid_cols)],
                    s1.at[0, p], s1.at[1, p], "fsdp", to,
                )
            )
        else:
            p1[pl.ds(m * grid_cols, grid_cols)] = acc.astype(bf16)
    lfirst = spread_first(leftf, left, d, ls)
    for c in out:
        c.wait_recv()
    out2 = []
    for p in range(members):
        to = lax.rem(m + p, members)
        for k in range(per_owner):
            keep = fill_ref[to * per_owner + k]
            for b in range(bands):
                got = p1[at_ref[(to * per_owner + k) * bands + b]]
                got = (got.astype(f32) * keep).astype(bf16)
                if p:
                    p2[to, k, b] = got
                else:
                    col[k, b, m] = got
        if p:
            out2.append(
                push(p2.at[to], col.at[:, :, m], s2.at[0, p], s2.at[1, p], "fsdp", to)
            )
    lrelay = spread_relay(leftf, width, d, ls, lfirst)
    for c in out2:
        c.wait_recv()
    mine = col.reshape(per_owner, block, width)
    gfirst = spread_first(gath, mine, d, gs)
    grelay = spread_relay(gath, width, d, gs, gfirst)
    for c in lrelay + grelay:
        c.wait_recv()
    for c in sums + out + out2 + list(lfirst[1:] + lrelay + gfirst[1:] + grelay):
        c.wait_send()
    lfirst[0].wait()
    gfirst[0].wait()


def bring(terms, left, at, fill):
    replicas, members, grid_cols, piece, width = terms.shape
    per_owner, block, _ = left.shape
    bands = block // (members * piece)
    bf16, dma = jnp.bfloat16, pltpu.SemaphoreType.DMA
    vmem = pl.BlockSpec(memory_space=pltpu.VMEM)
    smem = pl.BlockSpec(memory_space=pltpu.SMEM)
    full = jax.ShapeDtypeStruct((per_owner, block, replicas * width), bf16)
    return pl.pallas_call(
        functools.partial(bring_kernel, replicas, members),
        out_shape=(
            full, full,
            jax.ShapeDtypeStruct((per_owner, bands, members, piece, width), bf16),
        ),
        in_specs=[smem, smem, vmem, vmem],
        out_specs=(vmem, vmem, vmem),
        scratch_shapes=[
            pltpu.VMEM(terms.shape, bf16),
            pltpu.VMEM(terms.shape[1:], bf16),
            pltpu.VMEM((members * grid_cols, piece, width), bf16),
            pltpu.VMEM((members, per_owner, bands, piece, width), bf16),
            dma((2, replicas)), dma((2, members)), dma((2, members)), dma((3, 4)), dma((3, 4)),
        ],
        compiler_params=pltpu.CompilerParams(
            collective_id=0, has_side_effects=True, vmem_limit_bytes=40 * 2**20
        ),
    )(at, fill, terms, left)


def home_kernel(replicas, members, at_ref, partial, upd, inbox, bk, h1, p2, rs, s1, s2):
    d, m = lax.axis_index("dp"), lax.axis_index("fsdp")
    per_owner, bands = partial.shape[1:3]
    grid_cols = upd.shape[1]
    f32, bf16 = jnp.float32, jnp.bfloat16
    meet(replicas, members, d, m)
    sums, out, out2 = [], [], []
    for k in range(per_owner):
        for o in range(1, replicas):
            to = lax.rem(d + o, replicas)
            sums.append(
                push(partial.at[to, k], inbox.at[d, k], rs.at[0, k, o], rs.at[1, k, o], "dp", to)
            )
    for k in range(per_owner):
        for o in range(1, replicas):
            sums[k * (replicas - 1) + o - 1].wait_recv()
        for p in range(members):
            to = lax.rem(m + p, members)
            acc = partial[d, k, :, to].astype(f32)
            for o in range(1, replicas):
                acc += inbox[lax.rem(d + o, replicas), k, :, to].astype(f32)
            if p:
                bk[k, to] = acc.astype(bf16)
                out.append(
                    push(
                        bk.at[k, to],
                        h1.at[pl.ds((m * per_owner + k) * bands, bands)],
                        s1.at[0, k, p], s1.at[1, k, p], "fsdp", to,
                    )
                )
            else:
                h1[pl.ds((m * per_owner + k) * bands, bands)] = acc.astype(bf16)
    for c in out:
        c.wait_recv()
    for p in range(members):
        to = lax.rem(m + p, members)
        for c in range(grid_cols):
            got = h1[at_ref[to * grid_cols + c]]
            if p:
                p2[to, c] = got
            else:
                upd[m, c] = got
        if p:
            out2.append(push(p2.at[to], upd.at[m], s2.at[0, p], s2.at[1, p], "fsdp", to))
    for c in out2:
        c.wait_recv()
    for c in sums + out + out2:
        c.wait_send()


def home(partial, at, grid_cols):
    replicas, per_owner, bands, members, piece, width = partial.shape
    bf16, dma = jnp.bfloat16, pltpu.SemaphoreType.DMA
    vmem = pl.BlockSpec(memory_space=pltpu.VMEM)
    return pl.pallas_call(
        functools.partial(home_kernel, replicas, members),
        out_shape=jax.ShapeDtypeStruct((members, grid_cols, piece, width), bf16),
        in_specs=[pl.BlockSpec(memory_space=pltpu.SMEM), vmem],
        out_specs=vmem,
        scratch_shapes=[
            pltpu.VMEM(partial.shape, bf16),
            pltpu.VMEM((per_owner, members, bands, piece, width), bf16),
            pltpu.VMEM((members * per_owner * bands, piece, width), bf16),
            pltpu.VMEM((members, grid_cols, piece, width), bf16),
            dma((2, per_owner, replicas)), dma((2, per_owner, members)), dma((2, members)),
        ],
        compiler_params=pltpu.CompilerParams(
            collective_id=1, has_side_effects=True, vmem_limit_bytes=40 * 2**20
        ),
    )(at, partial)


def slot_lookup_table(block_owner_index, block_grid_cell, slot_count, per_owner):
    block_ids = jnp.arange(block_owner_index.shape[0], dtype=jnp.int32)
    shared = (block_owner_index[:, None] == block_owner_index[None, :]) & (
        block_ids[None, :] < block_ids[:, None]
    )
    rank_in = jnp.sum(shared.astype(jnp.int32), axis=1)
    block_slot_index = block_owner_index * per_owner + rank_in
    slot_ids = jnp.arange(slot_count, dtype=jnp.int32)
    matches = (block_slot_index[None, :] == slot_ids[:, None]).astype(jnp.int32)
    filled_marker = jnp.sum(matches, axis=1)
    slot_grid_cell = jnp.sum(matches * block_grid_cell[None, :], axis=1)
    return (block_slot_index, filled_marker, slot_grid_cell)


def local(
    gradient,
    block_owner_index,
    block_grid_cell,
    left_eigen_basis,
    right_eigen_basis,
    left_statistic_matrix,
    right_statistic_matrix,
    first_adam_moment,
    second_adam_moment,
):
    bf16, f32 = jnp.bfloat16, jnp.float32
    replicas = lax.axis_size("dp")
    members = lax.axis_size("fsdp")
    member = lax.axis_index("fsdp")
    column_group = lax.axis_index("dp")
    per_owner, block, width = left_eigen_basis.shape
    band_rows, grid_cols = gradient.shape[1:3]
    bands = block // band_rows
    grid_rows = members // bands
    cells = grid_rows * grid_cols

    block_slot_index, filled_marker, slot_grid_cell = slot_lookup_table(
        block_owner_index, block_grid_cell, per_owner * members, per_owner
    )
    my_filled = lax.dynamic_slice_in_dim(filled_marker, member * per_owner, per_owner, 0)
    my_cell = lax.dynamic_slice_in_dim(slot_grid_cell, member * per_owner, per_owner, 0)

    left = left_eigen_basis.astype(bf16)
    right = right_eigen_basis.astype(bf16)
    piece_rows = band_rows // members
    direct = replicas == 4 and band_rows % members == 0 and piece_rows % 16 == 0
    if direct:
        terms = jnp.transpose(
            gradient.reshape(members, piece_rows, grid_cols, replicas, width), (3, 0, 2, 1, 4)
        )
        part = jnp.arange(bands, dtype=jnp.int32)[None, :]
        at = (
            (slot_grid_cell // grid_cols * bands)[:, None] + part
        ) * grid_cols + (slot_grid_cell % grid_cols)[:, None]
        gathered, left_full, col_piece = bring(
            terms, left, at.reshape(-1), (filled_marker > 0).astype(f32)
        )
        col_piece = col_piece.reshape(per_owner, block, width)
    else:
        left_full = lax.all_gather(left, "dp", axis=2, tiled=True)

        terms = jnp.transpose(
            gradient.reshape(band_rows, grid_cols, replicas, width), (2, 1, 0, 3)
        ).reshape(replicas * grid_cols * band_rows, width)
        reduced = lax.psum_scatter(terms, "dp", scatter_dimension=0, tiled=True)
        everyone = lax.all_gather(reduced, "fsdp", axis=0, tiled=True)
        everyone = everyone.reshape(grid_rows, bands, grid_cols, band_rows, width)
        pieces = []
        for k in range(per_owner):
            cell = my_cell[k]
            piece = lax.dynamic_slice(
                everyone,
                (cell // grid_cols, 0, cell % grid_cols, 0, 0),
                (1, bands, 1, band_rows, width),
            ).reshape(block, width)
            pieces.append(jnp.where(my_filled[k] > 0, piece, jnp.zeros_like(piece)))
        col_piece = jnp.stack(pieces)
        gathered = lax.all_gather(col_piece, "dp", axis=2, tiled=True)
    row_piece = lax.dynamic_slice_in_dim(gathered, column_group * width, width, 1)

    turned_right = jnp.einsum(
        "skj,sjc->skc", gathered, right, preferred_element_type=f32
    ).astype(bf16)
    turned = jnp.einsum("ski,skc->sic", left_full, turned_right, preferred_element_type=f32)
    new_first = 0.9 * first_adam_moment + 0.1 * turned
    new_second = 0.999 * second_adam_moment + 0.001 * turned * turned
    direction = (new_first / (jnp.sqrt(new_second) + 1e-08)).astype(bf16)
    mixed = jnp.einsum("sik,skc->sic", left_full, direction, preferred_element_type=f32).astype(bf16)
    partial = jnp.einsum(
        "sic,sdjc->dsij",
        mixed,
        right.reshape(per_owner, replicas, width, width),
        preferred_element_type=f32,
    ).astype(bf16)
    new_left = 0.95 * left_statistic_matrix + 0.05 * jnp.einsum(
        "sik,sjk->sij", gathered, row_piece, preferred_element_type=f32
    )
    new_right = 0.95 * right_statistic_matrix + 0.05 * jnp.einsum(
        "ski,skj->sij", gathered, col_piece, preferred_element_type=f32
    )

    if direct:
        all_cells = jnp.arange(cells, dtype=jnp.int32)
        hits = (block_grid_cell[None, :] == all_cells[:, None]).astype(jnp.int32)
        cell_slot = jnp.sum(hits * block_slot_index[None, :], axis=1)
        at = cell_slot.reshape(grid_rows, 1, grid_cols) * bands + jnp.arange(
            bands, dtype=jnp.int32
        ).reshape(1, bands, 1)
        mine = home(
            partial.reshape(replicas, per_owner, bands, members, piece_rows, width),
            at.reshape(-1),
            grid_cols,
        )
        update = jnp.transpose(mine, (0, 2, 1, 3)).reshape(band_rows, grid_cols, width)
    else:
        back = lax.psum_scatter(
            partial.reshape(replicas * per_owner * block, width), "dp", scatter_dimension=0, tiled=True
        ).reshape(per_owner, bands, band_rows, width)

        placed = []
        for cell in range(cells):
            here = jnp.zeros((bands, band_rows, width), bf16)
            for k in range(per_owner):
                here = jnp.where((my_filled[k] > 0) & (my_cell[k] == cell), back[k], here)
            placed.append(here)
        placed = jnp.stack(placed).reshape(grid_rows, grid_cols, bands, band_rows, width)
        placed = jnp.transpose(placed, (0, 2, 1, 3, 4)).reshape(members * grid_cols * band_rows, width)
        mine = lax.psum_scatter(placed, "fsdp", scatter_dimension=0, tiled=True)
        update = jnp.transpose(mine.reshape(grid_cols, band_rows, width), (1, 0, 2))
    return (new_left, new_right, new_first, new_second, update)


def solution(mesh):
    slots = P("fsdp", None, "dp")
    in_specs = (P("dp", "fsdp", None, None), P(), P()) + (slots,) * 6
    return jax.shard_map(
        local, mesh=mesh, in_specs=in_specs, out_specs=(slots,) * 5, check_vma=False
    )
```

time: 348 us -> 215 us (0.62); the launches traced: 348 us -> 211 us
  waiting for transfers between devices: 256 us -> 0 us
  Pallas kernels: 0 us -> 172 us
  between operations: 30.9 us -> 0.75 us
  local copies, waits for them, and re-layouts: 28.1 us -> 8.72 us
    pallas_call x0 -> x2, Pallas kernels: none -> 172 us  [the longest x1 102 us: bring(): pl.pallas_call(functools.partial(bring_kernel, replicas, members), out_sh...]
    all_gather x3 -> x0, waiting for transfers between devices: 139 us -> none  [the longest x1 55 us: local(): gathered = lax.all_gather(col_piece, 'dp', axis=2, tiled=True)]
    reduce_scatter x3 -> x0, waiting for transfers between devices: 117 us -> none  [the longest x1 42.5 us: local(): lax.psum_scatter(partial.reshape(replicas * per_owner * block, width), 'd...]
    unnamed x29 -> x13, local copies, waits for them, and re-layouts: 17.7 us -> 2.32 us
    transpose x2 -> x1, local copies, waits for them, and re-layouts: 4.61 us -> 0.04 us  [local(): jnp.transpose(mine, (0, 2, 1, 3)).reshape(band_rows, grid_cols, width)]
    reshape x0 -> x2, local copies, waits for them, and re-layouts: none -> 3.65 us  [local(): gradient.reshape(members, piece_rows, grid_cols, replicas, width)]
  transfers between devices with their start and end apart: 6 -> 0, of which waited for: 6 -> 0; matrix products, arithmetic and copies ran while one was open for 7% -> 0% of each run, Pallas kernels for 0% -> 0%
where the time goes in v2:
time: 215 us; the launch traced here: 211 us
  Pallas kernels  172 us (80%)
  matrix products  23 us (11%)
  local copies, waits for them, and re-layouts  8.72 us (4%)
  other arithmetic  6.05 us (3%)
    pallas_call x1, Pallas kernels, bring(): pl.pallas_call(functools.partial(bring_kernel, replicas, members), out_sh...  102 us
    pallas_call x1, Pallas kernels, home(): pl.pallas_call(functools.partial(home_kernel, replicas, members), out_sha...  70 us
    dot_general x1, matrix products, local(): jnp.einsum('ski,skc->sic', left_full, turned_right, preferred_element_typ...  9.37 us
    dot_general x1, matrix products, local(): jnp.einsum('sic,sdjc->dsij', mixed, right.reshape(per_owner, replicas, wi...  7.92 us

profile of v2, /device:TPU:0, one launch (start us, length us, event | category | flops | bytes accessed | tf_op | source)
XLA Modules:
  0.0 210.9 jit_solution(13534452688878510099)
XLA Ops:
  0.6 0.0 copy-start.2
  0.6 1.0 convert_reduce_fusion.1
  1.6 0.7 multiply_add_fusion.4
  2.3 0.8 select_reduce_fusion
  3.1 0.7 convert_reduce_fusion
  3.9 0.1 mul.110
  3.9 0.1 add.99.at_ref
  4.0 0.1 multiply_add_fusion.3
  4.1 0.1 add.90.at_ref
  4.2 2.7 %convert_element_type.35 = bf16[2,1024,256]{2,1,0:T(8,128)(2,1)} convert(f32[2,1024,256]{2,1,0:T(8,128)} %param.13) | non-fusion elementwise | flops 524288 | bytes 3145728 | tf_op jit(solution)/shard_map/convert_element_type | solution.py:271
  6.9 0.0 copy-done.2
  6.9 0.1 convert_element_type.34.left
  7.0 3.2 %reshape.89 = bf16[8,64,2,4,256]{4,3,2,1,0:T(4,128)(2,1)S(1)} reshape(bf16[1,512,2,1024]{3,2,1,0:T(2,128)(2,1)} %param.9) | data formatting | bytes 4194304 | tf_op jit(solution)/shard_map/reshape | solution.py:276
  10.1 0.5 copy.37
  10.6 0.0 copy-start.3
  10.7 102.3 %shard_map.128 = (bf16[2,1024,1024]{2,1,0:T(8,128)(2,1)S(1)}, bf16[2,1024,1024]{2,1,0:T(8,128)(2,1)S(1)}, bf16[2,2,8,64,256]{4,3,2,1,0:T(8,128)(2,1)S(1)}) custom-call(s32[32]{0:T(128)S(1)} %add.90.at_ref, f32[16]{0:T(128)S(1)} %compare_convert_fusion.fill_ref, bf16[4,8,2,64,256]{4,3,2,1,0:T(8,128)(2,1)S(1)} %bitcast.25, ...), custom_call_target="tpu_custom_call" | custom-call | tf_op jit(solution)/shard_map/pallas_call | solution.py:135
  113.0 0.0 copy-start
  113.0 0.0 copy-start.1
  113.0 0.0 copy-done.3
  113.0 0.0 copy-start.5
  113.0 3.1 %multiply_add_fusion.1 = f32[2,1024,256]{2,1,0:T(8,128)} fusion(f32[2,1024,256]{2,1,0:T(8,128)S(1)} %copy-done.3, bf16[2,1024,1024]{2,1,0:T(8,128)(2,1)S(1)} %get-tuple-element.8, bf16[2,1024,256]{2,1,0:T(8,128)(2,1)S(1)} %bitcast.27), kind=kOutput, calls=%fused_computation.6 | convolution fusion | flops 1075314688 | bytes 9437184 | tf_op jit(solution)/shard_map/ski,skj->sij/dot_general | solution.py:325
  116.1 0.0 copy-done
  116.1 1.0 copy-done.1
  117.1 0.0 copy-done.5
  117.1 0.0 copy-start.4
  117.1 2.7 %multiply_add_fusion.2 = f32[2,1024,256]{2,1,0:T(8,128)} fusion(f32[2,1024,256]{2,1,0:T(8,128)S(1)} %copy-done.5, bf16[2,1024,1024]{2,1,0:T(8,128)(2,1)S(1)} %get-tuple-element.8, s32[]{:T(128)S(6)} %select_n.25), kind=kOutput, calls=%fused_computation.7 | convolution fusion | flops 1075314688 | bytes 9437188 | tf_op jit(solution)/shard_map/sik,sjk->sij/dot_general | solution.py:322
  119.8 0.0 copy-done.4
  119.8 9.4 %fusion = (f32[2,1024,256]{2,1,0:T(8,128)}, f32[2,1024,256]{2,1,0:T(8,128)}) fusion(f32[2,1024,256]{2,1,0:T(8,128)} %param.17, f32[2,1024,256]{2,1,0:T(8,128)} %param.16, bf16[2,1024,1024]{2,1,0:T(8,128)(2,1)} %copy-done.1, bf16[2,1024,1024]{2,1,0:T(8,128)(2,1)} %copy-done, bf16[2,1024,256]{2,1,0:T(8,128)(2,1)S(1)} %copy-done.4), kind=kOutput, calls=%fused_computation.2 | convolution fusion | flops 2151677952 | bytes 17825792 | tf_op jit(solution)/shard_map/ski,skc->sic/dot_general | solution.py:311
  129.1 7.9 %convert_bitcast_fusion = bf16[4,2,1024,256]{3,2,0,1:T(8,128)(2,1)} fusion(bf16[2,4,256,256]{3,2,1,0:T(8,128)(2,1)S(1)} %bitcast.29, bf16[2,1024,1024]{2,1,0:T(8,128)(2,1)} %copy-done.1, f32[2,1024,256]{2,1,0:T(8,128)} %get-tuple-element.24, f32[2,1024,256]{2,1,0:T(8,128)} %get-tuple-element.23), kind=kOutput, calls=%fused_computation | convolution fusion | flops 2151677952 | bytes 13631488 | tf_op jit(solution)/shard_map/sic,sdjc->dsij/dot_general | solution.py:316
  137.0 2.5 %copy.28 = bf16[4,2,1024,256]{3,2,1,0:T(8,128)(2,1)S(1)} copy(bf16[4,2,1024,256]{3,2,0,1:T(8,128)(2,1)} %convert_bitcast_fusion) | data formatting | bytes 8388608 | tf_op jit(solution)/shard_map/convert_element_type | solution.py:321
  139.5 70.0 %shard_map.129 = bf16[8,2,64,256]{3,2,1,0:T(8,128)(2,1)S(1)} custom-call(s32[16]{0:T(128)S(1)} %add.99.at_ref, bf16[4,2,2,8,64,256]{5,4,3,2,1,0:T(8,128)(2,1)S(1)} %bitcast.24), custom_call_target="tpu_custom_call" | custom-call | tf_op jit(solution)/shard_map/pallas_call | solution.py:210
  209.5 1.3 copy.30
  (5 shorter events, 0.1 us)
Async XLA Ops:
  0.6 6.2 %copy-start.2 = (f32[2,1024,256]{2,1,0:T(8,128)S(1)}, f32[2,1024,256]{2,1,0:T(8,128)}, u32[]{:S(2)}) copy-start(f32[2,1024,256]{2,1,0:T(8,128)} %param.12) | copy-start | bytes 6291460
  10.6 102.4 %copy-start.3 = (f32[2,1024,256]{2,1,0:T(8,128)S(1)}, f32[2,1024,256]{2,1,0:T(8,128)}, u32[]{:S(2)}) copy-start(f32[2,1024,256]{2,1,0:T(8,128)} %param.15) | copy-start | bytes 6291460
  113.0 3.1 %copy-start = (bf16[2,1024,1024]{2,1,0:T(8,128)(2,1)}, bf16[2,1024,1024]{2,1,0:T(8,128)(2,1)S(1)}, u32[]{:S(2)}) copy-start(bf16[2,1024,1024]{2,1,0:T(8,128)(2,1)S(1)} %get-tuple-element.8) | copy-start | bytes 12582916
  113.0 4.1 %copy-start.1 = (bf16[2,1024,1024]{2,1,0:T(8,128)(2,1)}, bf16[2,1024,1024]{2,1,0:T(8,128)(2,1)S(1)}, u32[]{:S(2)}) copy-start(bf16[2,1024,1024]{2,1,0:T(8,128)(2,1)S(1)} %get-tuple-element.10) | copy-start | bytes 12582916
  113.0 4.0 %copy-start.5 = (f32[2,1024,256]{2,1,0:T(8,128)S(1)}, f32[2,1024,256]{2,1,0:T(8,128)}, u32[]{:S(2)}) copy-start(f32[2,1024,256]{2,1,0:T(8,128)} %param.14) | copy-start | bytes 6291460
  117.1 2.7 %copy-start.4 = (bf16[2,1024,256]{2,1,0:T(8,128)(2,1)S(1)}, bf16[2,1024,256]{2,1,0:T(8,128)(2,1)}, u32[]{:S(2)}) copy-start(bf16[2,1024,256]{2,1,0:T(8,128)(2,1)} %convert_element_type.35) | copy-start | bytes 3145732

commit v3 on v2

--- a/solution.py
+++ b/solution.py
@@ -60,8 +60,8 @@
 
 
 def bring_kernel(
-    replicas, members, at_ref, fill_ref, terms, left, gath, leftf, col,
-    inbox, red, p1, p2, rs, s1, s2, gs, ls,
+    replicas, members, at_ref, fill_ref, terms, left, gath, leftf,
+    col, inbox, red, p1, p2, rs, s1, s2, gs, ls,
 ):
     d, m = lax.axis_index("dp"), lax.axis_index("fsdp")
     per_owner, block, width = left.shape
@@ -134,13 +134,11 @@
     full = jax.ShapeDtypeStruct((per_owner, block, replicas * width), bf16)
     return pl.pallas_call(
         functools.partial(bring_kernel, replicas, members),
-        out_shape=(
-            full, full,
-            jax.ShapeDtypeStruct((per_owner, bands, members, piece, width), bf16),
-        ),
+        out_shape=(full, full),
         in_specs=[smem, smem, vmem, vmem],
-        out_specs=(vmem, vmem, vmem),
+        out_specs=(vmem, vmem),
         scratch_shapes=[
+            pltpu.VMEM((per_owner, bands, members, piece, width), bf16),
             pltpu.VMEM(terms.shape, bf16),
             pltpu.VMEM(terms.shape[1:], bf16),
             pltpu.VMEM((members * grid_cols, piece, width), bf16),
@@ -153,38 +151,135 @@
     )(at, fill, terms, left)
 
 
-def home_kernel(replicas, members, at_ref, partial, upd, inbox, bk, h1, p2, rs, s1, s2):
+def home_kernel(
+    replicas, members, at_ref, gath, leftf, right, lstat, rstat, first, second,
+    new_left, new_right, new_first, new_second, upd,
+    rf, rb, tr, dr, partial, ina, inb, rel, ina2, inb2, bk, h1, p2, ld, rs, s1, s2,
+):
     d, m = lax.axis_index("dp"), lax.axis_index("fsdp")
-    per_owner, bands = partial.shape[1:3]
-    grid_cols = upd.shape[1]
+    per_owner, block, width = right.shape
+    grid_cols, piece = upd.shape[1:3]
+    bands = block // (members * piece)
+    hb, half = bands // 2, block // 2
     f32, bf16 = jnp.float32, jnp.bfloat16
+    d1 = d + 1 - 2 * lax.rem(d, 2)
+    d2 = lax.rem(d + 2, 4)
+    d3 = 3 - d
+    loads = [
+        pltpu.make_async_copy(s, t, ld.at[i])
+        for i, (s, t) in enumerate(
+            (
+                (right, rf), (first, new_first), (second, new_second),
+                (lstat, new_left), (rstat, new_right),
+            )
+        )
+    ]
+    for c in loads:
+        c.start()
     meet(replicas, members, d, m)
-    sums, out, out2 = [], [], []
+    tiles = block // width
+    mine = pl.ds(pl.multiple_of(d * width, width), width)
+
+    def mul(x, y, dims):
+        return lax.dot_general(x, y, (dims, ((), ())), preferred_element_type=f32)
+
+    def tile(i):
+        return pl.ds(pl.multiple_of(i * width, width), width)
+
+    def turn(k):
+        @pl.loop(0, tiles)
+        def _(i):
+            tr[tile(i)] = mul(gath[k, tile(i)], rb[k], ((1,), (0,))).astype(bf16)
+
+        @pl.loop(0, tiles)
+        def _(i):
+            t = mul(leftf[k, :, tile(i)], tr[...], ((0,), (0,)))
+            nf = 0.9 * new_first[k, tile(i)] + 0.1 * t
+            ns = 0.999 * new_second[k, tile(i)] + 0.001 * t * t
+            new_first[k, tile(i)] = nf
+            new_second[k, tile(i)] = ns
+            dr[tile(i)] = (nf / (jnp.sqrt(ns) + 1e-08)).astype(bf16)
+
+        @pl.loop(0, tiles)
+        def _(i):
+            x = mul(leftf[k, tile(i)], dr[...], ((1,), (0,))).astype(bf16)
+            for t in range(replicas):
+                partial[t, k, tile(i)] = mul(
+                    x, rb[k, t * width : (t + 1) * width], ((1,), (1,))
+                ).astype(bf16)
+
+    def stats(k):
+        @pl.loop(0, tiles)
+        def _(i):
+            a = mul(gath[k, tile(i)], gath[k, mine], ((1,), (1,)))
+            new_left[k, tile(i)] = 0.95 * new_left[k, tile(i)] + 0.05 * a
+            c = mul(gath[k, :, tile(i)], gath[k, :, mine], ((0,), (0,)))
+            new_right[k, tile(i)] = 0.95 * new_right[k, tile(i)] + 0.05 * c
+
+    top, low = pl.ds(0, half), pl.ds(half, half)
+
+    def launch(k):
+        return [
+            push(partial.at[d3, k, top], ina.at[k, 1], rs.at[0, k, 0], rs.at[1, k, 0], "dp", d1),
+            push(partial.at[d3, k, low], inb.at[k, 1], rs.at[0, k, 1], rs.at[1, k, 1], "dp", d2),
+            push(partial.at[d1, k, top], ina.at[k, 0], rs.at[0, k, 2], rs.at[1, k, 2], "dp", d1),
+            push(partial.at[d2, k, low], inb.at[k, 0], rs.at[0, k, 3], rs.at[1, k, 3], "dp", d2),
+        ]
+
+    def relay(k, c):
+        c[0].wait_recv()
+        rel[k, 0] = (partial[d2, k, top].astype(f32) + ina[k, 1].astype(f32)).astype(bf16)
+        a = push(rel.at[k, 0], ina2.at[k], rs.at[0, k, 4], rs.at[1, k, 4], "dp", d2)
+        c[1].wait_recv()
+        rel[k, 1] = (partial[d1, k, low].astype(f32) + inb[k, 1].astype(f32)).astype(bf16)
+        b = push(rel.at[k, 1], inb2.at[k], rs.at[0, k, 5], rs.at[1, k, 5], "dp", d1)
+        return [a, b]
+
+    out, out2 = [], []
+
+    def finish(k, c, r):
+        for h in range(2):
+            c[2 + h].wait_recv()
+            r[h].wait_recv()
+            near, far = ((ina, ina2), (inb, inb2))[h]
+            for p in range(members):
+                to = lax.rem(m + p, members)
+                at = (m * per_owner + k) * bands + h * hb
+                for q in range(hb):
+                    row = pl.ds(pl.multiple_of((q * members + to) * piece, piece), piece)
+                    own = pl.ds(pl.multiple_of(h * half + (q * members + to) * piece, piece), piece)
+                    acc = (
+                        partial[d, k, own].astype(f32)
+                        + near[k, 0, row].astype(f32)
+                        + far[k, row].astype(f32)
+                    ).astype(bf16)
+                    if p:
+                        bk[k, h, to, q] = acc
+                    else:
+                        h1[at + q] = acc
+                if p:
+                    out.append(
+                        push(
+                            bk.at[k, h, to], h1.at[pl.ds(at, hb)],
+                            s1.at[0, k, h, p], s1.at[1, k, h, p], "fsdp", to,
+                        )
+                    )
+
+    loads[0].wait()
+    rb[...] = rf[...].astype(bf16)
+    loads[1].wait()
+    loads[2].wait()
+    sent, passed = [], []
     for k in range(per_owner):
-        for o in range(1, replicas):
-            to = lax.rem(d + o, replicas)
-            sums.append(
-                push(partial.at[to, k], inbox.at[d, k], rs.at[0, k, o], rs.at[1, k, o], "dp", to)
-            )
+        turn(k)
+        sent.append(launch(k))
+    loads[3].wait()
+    loads[4].wait()
     for k in range(per_owner):
-        for o in range(1, replicas):
-            sums[k * (replicas - 1) + o - 1].wait_recv()
-        for p in range(members):
-            to = lax.rem(m + p, members)
-            acc = partial[d, k, :, to].astype(f32)
-            for o in range(1, replicas):
-                acc += inbox[lax.rem(d + o, replicas), k, :, to].astype(f32)
-            if p:
-                bk[k, to] = acc.astype(bf16)
-                out.append(
-                    push(
-                        bk.at[k, to],
-                        h1.at[pl.ds((m * per_owner + k) * bands, bands)],
-                        s1.at[0, k, p], s1.at[1, k, p], "fsdp", to,
-                    )
-                )
-            else:
-                h1[pl.ds((m * per_owner + k) * bands, bands)] = acc.astype(bf16)
+        stats(k)
+        passed.append(relay(k, sent[k]))
+    for k in range(per_owner):
+        finish(k, sent[k], passed[k])
     for c in out:
         c.wait_recv()
     for p in range(members):
@@ -199,30 +294,44 @@
             out2.append(push(p2.at[to], upd.at[m], s2.at[0, p], s2.at[1, p], "fsdp", to))
     for c in out2:
         c.wait_recv()
-    for c in sums + out + out2:
+    for c in sum(sent + passed, []) + out + out2:
         c.wait_send()
 
 
-def home(partial, at, grid_cols):
-    replicas, per_owner, bands, members, piece, width = partial.shape
-    bf16, dma = jnp.bfloat16, pltpu.SemaphoreType.DMA
+def home(at, gath, leftf, right, lstat, rstat, first, second, replicas, members, grid_cols, piece):
+    per_owner, block, width = right.shape
+    bands = block // (members * piece)
+    bf16, f32, dma = jnp.bfloat16, jnp.float32, pltpu.SemaphoreType.DMA
     vmem = pl.BlockSpec(memory_space=pltpu.VMEM)
+    whole = pl.BlockSpec(memory_space=pl.ANY)
+    state = jax.ShapeDtypeStruct(right.shape, f32)
+    half = (per_owner, 2, block // 2, width)
     return pl.pallas_call(
         functools.partial(home_kernel, replicas, members),
-        out_shape=jax.ShapeDtypeStruct((members, grid_cols, piece, width), bf16),
-        in_specs=[pl.BlockSpec(memory_space=pltpu.SMEM), vmem],
-        out_specs=vmem,
+        out_shape=(state,) * 4
+        + (jax.ShapeDtypeStruct((members, grid_cols, piece, width), bf16),),
+        in_specs=[pl.BlockSpec(memory_space=pltpu.SMEM), vmem, vmem] + [whole] * 5,
+        out_specs=(vmem,) * 5,
         scratch_shapes=[
-            pltpu.VMEM(partial.shape, bf16),
-            pltpu.VMEM((per_owner, members, bands, piece, width), bf16),
+            pltpu.VMEM(right.shape, f32),
+            pltpu.VMEM(right.shape, bf16),
+            pltpu.VMEM((block, width), bf16),
+            pltpu.VMEM((block, width), bf16),
+            pltpu.VMEM((replicas, per_owner, block, width), bf16),
+            pltpu.VMEM(half, bf16),
+            pltpu.VMEM(half, bf16),
+            pltpu.VMEM(half, bf16),
+            pltpu.VMEM((per_owner, block // 2, width), bf16),
+            pltpu.VMEM((per_owner, block // 2, width), bf16),
+            pltpu.VMEM((per_owner, 2, members, bands // 2, piece, width), bf16),
             pltpu.VMEM((members * per_owner * bands, piece, width), bf16),
             pltpu.VMEM((members, grid_cols, piece, width), bf16),
-            dma((2, per_owner, replicas)), dma((2, per_owner, members)), dma((2, members)),
+            dma((5,)), dma((2, per_owner, 6)), dma((2, per_owner, 2, members)), dma((2, members)),
         ],
         compiler_params=pltpu.CompilerParams(
-            collective_id=1, has_side_effects=True, vmem_limit_bytes=40 * 2**20
+            collective_id=1, has_side_effects=True, vmem_limit_bytes=48 * 2**20
         ),
-    )(at, partial)
+    )(at, gath, leftf, right, lstat, rstat, first, second)
 
 
 def slot_lookup_table(block_owner_index, block_grid_cell, slot_count, per_owner):
@@ -270,7 +379,9 @@
     left = left_eigen_basis.astype(bf16)
     right = right_eigen_basis.astype(bf16)
     piece_rows = band_rows // members
-    direct = replicas == 4 and band_rows % members == 0 and piece_rows % 16 == 0
+    direct = (
+        replicas == 4 and bands % 2 == 0 and band_rows % members == 0 and piece_rows % 16 == 0
+    )
     if direct:
         terms = jnp.transpose(
             gradient.reshape(members, piece_rows, grid_cols, replicas, width), (3, 0, 2, 1, 4)
@@ -279,30 +390,50 @@
         at = (
             (slot_grid_cell // grid_cols * bands)[:, None] + part
         ) * grid_cols + (slot_grid_cell % grid_cols)[:, None]
-        gathered, left_full, col_piece = bring(
+        gathered, left_full = bring(
             terms, left, at.reshape(-1), (filled_marker > 0).astype(f32)
         )
-        col_piece = col_piece.reshape(per_owner, block, width)
-    else:
-        left_full = lax.all_gather(left, "dp", axis=2, tiled=True)
-
-        terms = jnp.transpose(
-            gradient.reshape(band_rows, grid_cols, replicas, width), (2, 1, 0, 3)
-        ).reshape(replicas * grid_cols * band_rows, width)
-        reduced = lax.psum_scatter(terms, "dp", scatter_dimension=0, tiled=True)
-        everyone = lax.all_gather(reduced, "fsdp", axis=0, tiled=True)
-        everyone = everyone.reshape(grid_rows, bands, grid_cols, band_rows, width)
-        pieces = []
-        for k in range(per_owner):
-            cell = my_cell[k]
-            piece = lax.dynamic_slice(
-                everyone,
-                (cell // grid_cols, 0, cell % grid_cols, 0, 0),
-                (1, bands, 1, band_rows, width),
-            ).reshape(block, width)
-            pieces.append(jnp.where(my_filled[k] > 0, piece, jnp.zeros_like(piece)))
-        col_piece = jnp.stack(pieces)
-        gathered = lax.all_gather(col_piece, "dp", axis=2, tiled=True)
+        all_cells = jnp.arange(cells, dtype=jnp.int32)
+        hits = (block_grid_cell[None, :] == all_cells[:, None]).astype(jnp.int32)
+        cell_slot = jnp.sum(hits * block_slot_index[None, :], axis=1)
+        at = cell_slot.reshape(grid_rows, 1, grid_cols) * bands + jnp.arange(
+            bands, dtype=jnp.int32
+        ).reshape(1, bands, 1)
+        *states, mine = home(
+            at.reshape(-1),
+            gathered,
+            left_full,
+            right_eigen_basis,
+            left_statistic_matrix,
+            right_statistic_matrix,
+            first_adam_moment,
+            second_adam_moment,
+            replicas,
+            members,
+            grid_cols,
+            piece_rows,
+        )
+        update = jnp.transpose(mine, (0, 2, 1, 3)).reshape(band_rows, grid_cols, width)
+        return (*states, update)
+    left_full = lax.all_gather(left, "dp", axis=2, tiled=True)
+
+    terms = jnp.transpose(
+        gradient.reshape(band_rows, grid_cols, replicas, width), (2, 1, 0, 3)
+    ).reshape(replicas * grid_cols * band_rows, width)
+    reduced = lax.psum_scatter(terms, "dp", scatter_dimension=0, tiled=True)
+    everyone = lax.all_gather(reduced, "fsdp", axis=0, tiled=True)
+    everyone = everyone.reshape(grid_rows, bands, grid_cols, band_rows, width)
+    pieces = []
+    for k in range(per_owner):
+        cell = my_cell[k]
+        piece = lax.dynamic_slice(
+            everyone,
+            (cell // grid_cols, 0, cell % grid_cols, 0, 0),
+            (1, bands, 1, band_rows, width),
+        ).reshape(block, width)
+        pieces.append(jnp.where(my_filled[k] > 0, piece, jnp.zeros_like(piece)))
+    col_piece = jnp.stack(pieces)
+    gathered = lax.all_gather(col_piece, "dp", axis=2, tiled=True)
     row_piece = lax.dynamic_slice_in_dim(gathered, column_group * width, width, 1)
 
     turned_right = jnp.einsum(
@@ -326,34 +457,20 @@
         "ski,skj->sij", gathered, col_piece, preferred_element_type=f32
     )
 
-    if direct:
-        all_cells = jnp.arange(cells, dtype=jnp.int32)
-        hits = (block_grid_cell[None, :] == all_cells[:, None]).astype(jnp.int32)
-        cell_slot = jnp.sum(hits * block_slot_index[None, :], axis=1)
-        at = cell_slot.reshape(grid_rows, 1, grid_cols) * bands + jnp.arange(
-            bands, dtype=jnp.int32
-        ).reshape(1, bands, 1)
-        mine = home(
-            partial.reshape(replicas, per_owner, bands, members, piece_rows, width),
-            at.reshape(-1),
-            grid_cols,
-        )
-        update = jnp.transpose(mine, (0, 2, 1, 3)).reshape(band_rows, grid_cols, width)
-    else:
-        back = lax.psum_scatter(
-            partial.reshape(replicas * per_owner * block, width), "dp", scatter_dimension=0, tiled=True
-        ).reshape(per_owner, bands, band_rows, width)
-
-        placed = []
-        for cell in range(cells):
-            here = jnp.zeros((bands, band_rows, width), bf16)
-            for k in range(per_owner):
-                here = jnp.where((my_filled[k] > 0) & (my_cell[k] == cell), back[k], here)
-            placed.append(here)
-        placed = jnp.stack(placed).reshape(grid_rows, grid_cols, bands, band_rows, width)
-        placed = jnp.transpose(placed, (0, 2, 1, 3, 4)).reshape(members * grid_cols * band_rows, width)
-        mine = lax.psum_scatter(placed, "fsdp", scatter_dimension=0, tiled=True)
-        update = jnp.transpose(mine.reshape(grid_cols, band_rows, width), (1, 0, 2))
+    back = lax.psum_scatter(
+        partial.reshape(replicas * per_owner * block, width), "dp", scatter_dimension=0, tiled=True
+    ).reshape(per_owner, bands, band_rows, width)
+
+    placed = []
+    for cell in range(cells):
+        here = jnp.zeros((bands, band_rows, width), bf16)
+        for k in range(per_owner):
+            here = jnp.where((my_filled[k] > 0) & (my_cell[k] == cell), back[k], here)
+        placed.append(here)
+    placed = jnp.stack(placed).reshape(grid_rows, grid_cols, bands, band_rows, width)
+    placed = jnp.transpose(placed, (0, 2, 1, 3, 4)).reshape(members * grid_cols * band_rows, width)
+    mine = lax.psum_scatter(placed, "fsdp", scatter_dimension=0, tiled=True)
+    update = jnp.transpose(mine.reshape(grid_cols, band_rows, width), (1, 0, 2))
     return (new_left, new_right, new_first, new_second, update)
 
 

time: 215 us -> 204 us (0.949); the launches traced: 211 us -> 202 us
  matrix products: 23 us -> 0 us
  Pallas kernels: 172 us -> 180 us
  local copies, waits for them, and re-layouts: 8.72 us -> 16.5 us
    dot_general x4 -> x0, matrix products: 23 us -> none  [the longest x1 9.37 us: local(): jnp.einsum('ski,skc->sic', left_full, turned_right, preferred_element_typ...]
    unnamed x13, local copies, waits for them, and re-layouts: 2.32 us -> 12.6 us
    pallas_call x1, Pallas kernels: 70 us -> 77.9 us  [home(): pl.pallas_call(functools.partial(home_kernel, replicas, members), out_sha...]
    convert_element_type x1 -> x0, other arithmetic: 2.67 us -> none  [local(): right = right_eigen_basis.astype(bf16)]
    convert_element_type x1 -> x0, local copies, waits for them, and re-layouts: 2.46 us -> none  [local(): partial = jnp.einsum('sic,sdjc->dsij', mixed, right.reshape(per_owner, re...]
where the time goes in v3:
time: 204 us; the launch traced here: 202 us
  Pallas kernels  180 us (88%)
  local copies, waits for them, and re-layouts  16.5 us (8%)
  other arithmetic  4.89 us (2%)
    pallas_call x1, Pallas kernels, bring(): pl.pallas_call(functools.partial(bring_kernel, replicas, members), out_sh...  102 us
    pallas_call x1, Pallas kernels, home(): pl.pallas_call(functools.partial(home_kernel, replicas, members), out_sha...  77.9 us
    unnamed x13, local copies, waits for them, and re-layouts  12.6 us

profile of v3, /device:TPU:0, one launch (start us, length us, event | category | flops | bytes accessed | tf_op | source)
XLA Modules:
  0.0 202.3 jit_solution(1037443900501492300)
XLA Ops:
  0.6 0.9 convert_reduce_fusion.1
  1.5 0.7 multiply_add_fusion.1
  2.2 0.8 select_reduce_fusion.1
  3.0 0.7 convert_reduce_fusion
  3.8 0.1 mul.49
  3.8 0.1 add.66.at_ref
  3.9 0.1 multiply_add_fusion
  4.0 0.1 add.73.at_ref
  4.1 1.7 convert_element_type.16.left
  5.8 3.2 %reshape.76 = bf16[8,64,2,4,256]{4,3,2,1,0:T(4,128)(2,1)S(1)} reshape(bf16[1,512,2,1024]{3,2,1,0:T(2,128)(2,1)} %param.9) | data formatting | bytes 4194304 | tf_op jit(solution)/shard_map/reshape | solution.py:387
  9.0 0.5 copy.25
  9.5 102.3 %shard_map.128 = (bf16[2,1024,1024]{2,1,0:T(8,128)(2,1)S(1)}, bf16[2,1024,1024]{2,1,0:T(8,128)(2,1)S(1)}) custom-call(s32[32]{0:T(128)S(1)} %add.73.at_ref, f32[16]{0:T(128)S(1)} %compare_convert_fusion.fill_ref, bf16[4,8,2,64,256]{4,3,2,1,0:T(8,128)(2,1)S(1)} %bitcast.5, bf16[2,1024,256]{2,1,0:T(8,128)(2,1)S(1)} %convert_element_type.16.left), custom_call_target="tpu_custom_call" | custom-call | tf_op jit(solution)/shard_map/pallas_call | solution.py:135
  111.8 0.0 copy-start
  111.8 1.9 copy-done
  113.7 0.0 copy-start.1
  113.7 2.0 copy-done.1
  115.7 77.9 %shard_map.129 = (f32[2,1024,256]{2,1,0:T(8,128)S(1)}, f32[2,1024,256]{2,1,0:T(8,128)S(1)}, f32[2,1024,256]{2,1,0:T(8,128)}, f32[2,1024,256]{2,1,0:T(8,128)}, bf16[8,2,64,256]{3,2,1,0:T(8,128)(2,1)S(1)}) custom-call(s32[16]{0:T(128)S(1)} %add.66.at_ref, bf16[2,1024,1024]{2,1,0:T(8,128)(2,1)} %copy-done, bf16[2,1024,1024]{2,1,0:T(8,128)(2,1)} %copy-done.1, ...), custom_call_target="tpu_custom_call" | custom-call | tf_op jit(solution)/shard_map/pallas_call | solution.py:309
  193.7 1.3 copy.21
  195.0 1.3 copy.30
  196.3 0.0 copy-start.3
  196.3 1.3 copy.31
  197.6 1.0 copy-done.3
  198.7 0.0 copy-start.2
  198.7 1.3 copy.32
  200.0 1.0 copy-done.2
  201.0 1.3 copy.33
  (5 shorter events, 0.1 us)
Async XLA Ops:
  111.8 1.9 copy-start
  113.7 2.0 copy-start.1
  196.3 2.3 %copy-start.3 = (f32[2,1024,256]{2,1,0:T(8,128)S(1)}, f32[2,1024,256]{2,1,0:T(8,128)}, u32[]{:S(2)}) copy-start(f32[2,1024,256]{2,1,0:T(8,128)} %get-tuple-element.40) | copy-start | bytes 6291460
  198.7 2.3 %copy-start.2 = (f32[2,1024,256]{2,1,0:T(8,128)S(1)}, f32[2,1024,256]{2,1,0:T(8,128)}, u32[]{:S(2)}) copy-start(f32[2,1024,256]{2,1,0:T(8,128)} %get-tuple-element.41) | copy-start | bytes 6291460

commit v4 on v3

--- a/solution.py
+++ b/solution.py
@@ -37,8 +37,8 @@
 
 
 def spread_first(full, mine, d, sems):
-    width = mine.shape[2]
-    here = full.at[:, :, pl.ds(pl.multiple_of(d * width, width), width)]
+    width = mine.shape[1]
+    here = full.at[:, pl.ds(pl.multiple_of(d * width, width), width)]
     own = pltpu.make_async_copy(mine, here, sems.at[2, 0])
     own.start()
     one = push(mine, here, sems.at[0, 0], sems.at[1, 0], "dp", d + 1 - 2 * lax.rem(d, 2))
@@ -47,114 +47,22 @@
 
 
 def spread_relay(full, width, d, sems, first):
-    half = full.shape[1] // 2
+    half = full.shape[0] // 2
     d1 = d + 1 - 2 * lax.rem(d, 2)
     d2 = lax.rem(d + 2, 4)
     first[1].wait_recv()
-    top = full.at[:, pl.ds(0, half), pl.ds(pl.multiple_of(d1 * width, width), width)]
+    top = full.at[pl.ds(0, half), pl.ds(pl.multiple_of(d1 * width, width), width)]
     a = push(top, top, sems.at[0, 2], sems.at[1, 2], "dp", d2)
     first[2].wait_recv()
-    low = full.at[:, pl.ds(half, half), pl.ds(pl.multiple_of(d2 * width, width), width)]
+    low = full.at[pl.ds(half, half), pl.ds(pl.multiple_of(d2 * width, width), width)]
     b = push(low, low, sems.at[0, 3], sems.at[1, 3], "dp", d1)
     return a, b
 
 
-def bring_kernel(
-    replicas, members, at_ref, fill_ref, terms, left, gath, leftf,
-    col, inbox, red, p1, p2, rs, s1, s2, gs, ls,
-):
-    d, m = lax.axis_index("dp"), lax.axis_index("fsdp")
-    per_owner, block, width = left.shape
-    grid_cols, piece = terms.shape[2:4]
-    bands = p2.shape[2]
-    f32, bf16 = jnp.float32, jnp.bfloat16
-    meet(replicas, members, d, m)
-    sums = []
-    for o in range(1, replicas):
-        to = lax.rem(d + o, replicas)
-        sums.append(push(terms.at[to], inbox.at[d], rs.at[0, o], rs.at[1, o], "dp", to))
-    for c in sums:
-        c.wait_recv()
-    out = []
-    for p in range(members):
-        to = lax.rem(m + p, members)
-        acc = terms[d, to].astype(f32)
-        for o in range(1, replicas):
-            acc += inbox[lax.rem(d + o, replicas), to].astype(f32)
-        if p:
-            red[to] = acc.astype(bf16)
-            out.append(
-                push(
-                    red.at[to], p1.at[pl.ds(m * grid_cols, grid_cols)],
-                    s1.at[0, p], s1.at[1, p], "fsdp", to,
-                )
-            )
-        else:
-            p1[pl.ds(m * grid_cols, grid_cols)] = acc.astype(bf16)
-    lfirst = spread_first(leftf, left, d, ls)
-    for c in out:
-        c.wait_recv()
-    out2 = []
-    for p in range(members):
-        to = lax.rem(m + p, members)
-        for k in range(per_owner):
-            keep = fill_ref[to * per_owner + k]
-            for b in range(bands):
-                got = p1[at_ref[(to * per_owner + k) * bands + b]]
-                got = (got.astype(f32) * keep).astype(bf16)
-                if p:
-                    p2[to, k, b] = got
-                else:
-                    col[k, b, m] = got
-        if p:
-            out2.append(
-                push(p2.at[to], col.at[:, :, m], s2.at[0, p], s2.at[1, p], "fsdp", to)
-            )
-    lrelay = spread_relay(leftf, width, d, ls, lfirst)
-    for c in out2:
-        c.wait_recv()
-    mine = col.reshape(per_owner, block, width)
-    gfirst = spread_first(gath, mine, d, gs)
-    grelay = spread_relay(gath, width, d, gs, gfirst)
-    for c in lrelay + grelay:
-        c.wait_recv()
-    for c in sums + out + out2 + list(lfirst[1:] + lrelay + gfirst[1:] + grelay):
-        c.wait_send()
-    lfirst[0].wait()
-    gfirst[0].wait()
-
-
-def bring(terms, left, at, fill):
-    replicas, members, grid_cols, piece, width = terms.shape
-    per_owner, block, _ = left.shape
-    bands = block // (members * piece)
-    bf16, dma = jnp.bfloat16, pltpu.SemaphoreType.DMA
-    vmem = pl.BlockSpec(memory_space=pltpu.VMEM)
-    smem = pl.BlockSpec(memory_space=pltpu.SMEM)
-    full = jax.ShapeDtypeStruct((per_owner, block, replicas * width), bf16)
-    return pl.pallas_call(
-        functools.partial(bring_kernel, replicas, members),
-        out_shape=(full, full),
-        in_specs=[smem, smem, vmem, vmem],
-        out_specs=(vmem, vmem),
-        scratch_shapes=[
-            pltpu.VMEM((per_owner, bands, members, piece, width), bf16),
-            pltpu.VMEM(terms.shape, bf16),
-            pltpu.VMEM(terms.shape[1:], bf16),
-            pltpu.VMEM((members * grid_cols, piece, width), bf16),
-            pltpu.VMEM((members, per_owner, bands, piece, width), bf16),
-            dma((2, replicas)), dma((2, members)), dma((2, members)), dma((3, 4)), dma((3, 4)),
-        ],
-        compiler_params=pltpu.CompilerParams(
-            collective_id=0, has_side_effects=True, vmem_limit_bytes=40 * 2**20
-        ),
-    )(at, fill, terms, left)
-
-
-def home_kernel(
-    replicas, members, at_ref, gath, leftf, right, lstat, rstat, first, second,
+def step_kernel(
+    replicas, members, pick_ref, fill_ref, at_ref, terms, left, right, lstat, rstat, first, second,
     new_left, new_right, new_first, new_second, upd,
-    rf, rb, tr, dr, partial, ina, inb, rel, ina2, inb2, bk, h1, p2, ld, rs, s1, s2,
+    gath, leftf, col, xs, red, p1, p0, rs0, s0, g2, gs, ls, rf, rb, tr, dr, partial, ina, inb, rel, ina2, inb2, bk, h1, p2, ld, rs, s1, s2,
 ):
     d, m = lax.axis_index("dp"), lax.axis_index("fsdp")
     per_owner, block, width = right.shape
@@ -265,12 +173,78 @@
                         )
                     )
 
+    hm = members // 2
+    upper, lower = pl.ds(0, hm), pl.ds(hm, hm)
+    g = [
+        push(terms.at[d3, upper], xs.at[1, upper], rs0.at[0, 0], rs0.at[1, 0], "dp", d1),
+        push(terms.at[d3, lower], xs.at[1, lower], rs0.at[0, 1], rs0.at[1, 1], "dp", d2),
+        push(terms.at[d1, upper], xs.at[0, upper], rs0.at[0, 2], rs0.at[1, 2], "dp", d1),
+        push(terms.at[d2, lower], xs.at[0, lower], rs0.at[0, 3], rs0.at[1, 3], "dp", d2),
+    ]
+    g[0].wait_recv()
+    xs[2, upper] = (terms[d2, upper].astype(f32) + xs[1, upper].astype(f32)).astype(bf16)
+    g.append(push(xs.at[2, upper], xs.at[3, upper], rs0.at[0, 4], rs0.at[1, 4], "dp", d2))
+    g[1].wait_recv()
+    xs[2, lower] = (terms[d1, lower].astype(f32) + xs[1, lower].astype(f32)).astype(bf16)
+    g.append(push(xs.at[2, lower], xs.at[3, lower], rs0.at[0, 5], rs0.at[1, 5], "dp", d1))
+    for c in g[2:]:
+        c.wait_recv()
+    spread = []
+    for p in range(members):
+        to = lax.rem(m + p, members)
+        acc = terms[d, to].astype(f32) + xs[0, to].astype(f32) + xs[3, to].astype(f32)
+        here = pl.ds(m * grid_cols, grid_cols)
+        if p:
+            red[to] = acc.astype(bf16)
+            spread.append(push(red.at[to], p1.at[here], s0.at[0, p], s0.at[1, p], "fsdp", to))
+        else:
+            p1[here] = acc.astype(bf16)
+    lfirst = [spread_first(leftf.at[k], left.at[k], d, ls.at[k]) for k in range(per_owner)]
     loads[0].wait()
     rb[...] = rf[...].astype(bf16)
+    for c in spread:
+        c.wait_recv()
+    dealt = []
+    for k in range(per_owner):
+        dealt.append([])
+        for p in range(members):
+            to = lax.rem(m + p, members)
+            keep = fill_ref[to * per_owner + k]
+            for b in range(bands):
+                got = p1[pick_ref[(to * per_owner + k) * bands + b]]
+                got = (got.astype(f32) * keep).astype(bf16)
+                if p:
+                    p0[to, k, b] = got
+                else:
+                    col[k, b, m] = got
+            if p:
+                dealt[k].append(
+                    push(
+                        p0.at[to, k], col.at[k, :, m],
+                        g2.at[0, k, p], g2.at[1, k, p], "fsdp", to,
+                    )
+                )
+    lrelay = [
+        spread_relay(leftf.at[k], width, d, ls.at[k], lfirst[k]) for k in range(per_owner)
+    ]
+    gfirst = []
+    for k in range(per_owner):
+        for c in dealt[k]:
+            c.wait_recv()
+        gfirst.append(
+            spread_first(gath.at[k], col.at[k].reshape(block, width), d, gs.at[k])
+        )
+    grelay = [
+        spread_relay(gath.at[k], width, d, gs.at[k], gfirst[k]) for k in range(per_owner)
+    ]
     loads[1].wait()
     loads[2].wait()
     sent, passed = [], []
     for k in range(per_owner):
+        lfirst[k][0].wait()
+        gfirst[k][0].wait()
+        for c in lrelay[k] + grelay[k]:
+            c.wait_recv()
         turn(k)
         sent.append(launch(k))
     loads[3].wait()
@@ -294,12 +268,16 @@
             out2.append(push(p2.at[to], upd.at[m], s2.at[0, p], s2.at[1, p], "fsdp", to))
     for c in out2:
         c.wait_recv()
-    for c in sum(sent + passed, []) + out + out2:
+    for c in g + spread + sum(dealt + sent + passed, []) + out + out2:
         c.wait_send()
-
-
-def home(at, gath, leftf, right, lstat, rstat, first, second, replicas, members, grid_cols, piece):
+    for k in range(per_owner):
+        for c in lfirst[k][1:] + lrelay[k] + gfirst[k][1:] + grelay[k]:
+            c.wait_send()
+
+
+def step(pick, fill, at, terms, left, right, lstat, rstat, first, second):
     per_owner, block, width = right.shape
+    replicas, members, grid_cols, piece, _ = terms.shape
     bands = block // (members * piece)
     bf16, f32, dma = jnp.bfloat16, jnp.float32, pltpu.SemaphoreType.DMA
     vmem = pl.BlockSpec(memory_space=pltpu.VMEM)
@@ -307,12 +285,21 @@
     state = jax.ShapeDtypeStruct(right.shape, f32)
     half = (per_owner, 2, block // 2, width)
     return pl.pallas_call(
-        functools.partial(home_kernel, replicas, members),
+        functools.partial(step_kernel, replicas, members),
         out_shape=(state,) * 4
         + (jax.ShapeDtypeStruct((members, grid_cols, piece, width), bf16),),
-        in_specs=[pl.BlockSpec(memory_space=pltpu.SMEM), vmem, vmem] + [whole] * 5,
+        in_specs=[pl.BlockSpec(memory_space=pltpu.SMEM)] * 3 + [vmem] * 2 + [whole] * 5,
         out_specs=(vmem,) * 5,
         scratch_shapes=[
+            pltpu.VMEM((per_owner, block, replicas * width), bf16),
+            pltpu.VMEM((per_owner, block, replicas * width), bf16),
+            pltpu.VMEM((per_owner, bands, members, piece, width), bf16),
+            pltpu.VMEM((4,) + terms.shape[1:], bf16),
+            pltpu.VMEM(terms.shape[1:], bf16),
+            pltpu.VMEM((members * grid_cols, piece, width), bf16),
+            pltpu.VMEM((members, per_owner, bands, piece, width), bf16),
+            dma((2, 6)), dma((2, members)), dma((2, per_owner, members)),
+            dma((per_owner, 3, 4)), dma((per_owner, 3, 4)),
             pltpu.VMEM(right.shape, f32),
             pltpu.VMEM(right.shape, bf16),
             pltpu.VMEM((block, width), bf16),
@@ -329,9 +316,9 @@
             dma((5,)), dma((2, per_owner, 6)), dma((2, per_owner, 2, members)), dma((2, members)),
         ],
         compiler_params=pltpu.CompilerParams(
-            collective_id=1, has_side_effects=True, vmem_limit_bytes=48 * 2**20
+            collective_id=0, has_side_effects=True, vmem_limit_bytes=52 * 2**20
         ),
-    )(at, gath, leftf, right, lstat, rstat, first, second)
+    )(pick, fill, at, terms, left, right, lstat, rstat, first, second)
 
 
 def slot_lookup_table(block_owner_index, block_grid_cell, slot_count, per_owner):
@@ -380,38 +367,33 @@
     right = right_eigen_basis.astype(bf16)
     piece_rows = band_rows // members
     direct = (
-        replicas == 4 and bands % 2 == 0 and band_rows % members == 0 and piece_rows % 16 == 0
+        replicas == 4 and bands % 2 == members % 2 == 0 and band_rows % members == 0 and piece_rows % 16 == 0
     )
     if direct:
         terms = jnp.transpose(
             gradient.reshape(members, piece_rows, grid_cols, replicas, width), (3, 0, 2, 1, 4)
         )
         part = jnp.arange(bands, dtype=jnp.int32)[None, :]
-        at = (
+        pick = (
             (slot_grid_cell // grid_cols * bands)[:, None] + part
         ) * grid_cols + (slot_grid_cell % grid_cols)[:, None]
-        gathered, left_full = bring(
-            terms, left, at.reshape(-1), (filled_marker > 0).astype(f32)
-        )
         all_cells = jnp.arange(cells, dtype=jnp.int32)
         hits = (block_grid_cell[None, :] == all_cells[:, None]).astype(jnp.int32)
         cell_slot = jnp.sum(hits * block_slot_index[None, :], axis=1)
         at = cell_slot.reshape(grid_rows, 1, grid_cols) * bands + jnp.arange(
             bands, dtype=jnp.int32
         ).reshape(1, bands, 1)
-        *states, mine = home(
+        *states, mine = step(
+            pick.reshape(-1),
+            (filled_marker > 0).astype(f32),
             at.reshape(-1),
-            gathered,
-            left_full,
+            terms,
+            left,
             right_eigen_basis,
             left_statistic_matrix,
             right_statistic_matrix,
             first_adam_moment,
             second_adam_moment,
-            replicas,
-            members,
-            grid_cols,
-            piece_rows,
         )
         update = jnp.transpose(mine, (0, 2, 1, 3)).reshape(band_rows, grid_cols, width)
         return (*states, update)

time: 204 us -> 183 us (0.90)
  Pallas kernels: 180 us -> 160 us
    pallas_call x2 -> x1, Pallas kernels: 180 us -> 160 us  [step(): pl.pallas_call(functools.partial(step_kernel, replicas, members), out_sha...]
    unnamed x13, local copies, waits for them, and re-layouts: 12.6 us -> 9.95 us
where the time goes in v4:
time: 183 us; the launch traced here: 181 us
  Pallas kernels  160 us (87%)
  local copies, waits for them, and re-layouts  15.2 us (8%)
  other arithmetic  4.89 us (3%)
    pallas_call x1, Pallas kernels, step(): pl.pallas_call(functools.partial(step_kernel, replicas, members), out_sha...  160 us
    unnamed x13, local copies, waits for them, and re-layouts  9.95 us
    reshape x2, local copies, waits for them, and re-layouts, local(): gradient.reshape(members, piece_rows, grid_cols, replicas, width)  4.96 us

profile of v4, /device:TPU:0, one launch (start us, length us, event | category | flops | bytes accessed | tf_op | source)
XLA Modules:
  0.0 180.9 jit_solution(9061436794458414248)
XLA Ops:
  0.6 0.9 convert_reduce_fusion.1
  1.5 0.7 multiply_add_fusion.1
  2.2 0.8 select_reduce_fusion
  3.0 0.7 convert_reduce_fusion
  3.8 0.1 mul.54
  3.8 0.1 add.73.at_ref
  3.9 0.1 multiply_add_fusion
  4.0 0.1 add.69.pick_ref
  4.1 1.7 convert_element_type.16.left
  5.8 3.2 %reshape.76 = bf16[8,64,2,4,256]{4,3,2,1,0:T(4,128)(2,1)S(1)} reshape(bf16[1,512,2,1024]{3,2,1,0:T(2,128)(2,1)} %param.9) | data formatting | bytes 4194304 | tf_op jit(solution)/shard_map/reshape | solution.py:374
  9.0 1.8 copy.25
  10.8 160.1 %shard_map.128 = (f32[2,1024,256]{2,1,0:T(8,128)}, f32[2,1024,256]{2,1,0:T(8,128)}, f32[2,1024,256]{2,1,0:T(8,128)}, f32[2,1024,256]{2,1,0:T(8,128)}, bf16[8,2,64,256]{3,2,1,0:T(8,128)(2,1)S(1)}) custom-call(s32[32]{0:T(128)S(1)} %add.69.pick_ref, f32[16]{0:T(128)S(1)} %compare_convert_fusion.fill_ref, s32[16]{0:T(128)S(1)} %add.73.at_ref, ...), custom_call_target="tpu_custom_call" | custom-call | tf_op jit(solution)/shard_map/pallas_call | solution.py:287
  170.9 0.0 copy-start.3
  171.0 1.3 copy.21
  172.3 0.3 copy-done.3
  172.6 0.0 copy-start.2
  172.6 1.3 copy.30
  173.9 1.0 copy-done.2
  174.9 0.0 copy-start.1
  174.9 1.3 copy.31
  176.2 1.0 copy-done.1
  177.3 0.0 copy-start
  177.3 1.3 copy.32
  178.6 1.0 copy-done
  179.6 1.3 copy.33
  (5 shorter events, 0.1 us)
Async XLA Ops:
  170.9 1.6 copy-start.3
  172.6 2.3 %copy-start.2 = (f32[2,1024,256]{2,1,0:T(8,128)S(1)}, f32[2,1024,256]{2,1,0:T(8,128)}, u32[]{:S(2)}) copy-start(f32[2,1024,256]{2,1,0:T(8,128)} %get-tuple-element.35) | copy-start | bytes 6291460
  174.9 2.3 %copy-start.1 = (f32[2,1024,256]{2,1,0:T(8,128)S(1)}, f32[2,1024,256]{2,1,0:T(8,128)}, u32[]{:S(2)}) copy-start(f32[2,1024,256]{2,1,0:T(8,128)} %get-tuple-element.36) | copy-start | bytes 6291460
  177.3 2.3 %copy-start = (f32[2,1024,256]{2,1,0:T(8,128)S(1)}, f32[2,1024,256]{2,1,0:T(8,128)}, u32[]{:S(2)}) copy-start(f32[2,1024,256]{2,1,0:T(8,128)} %get-tuple-element.37) | copy-start | bytes 6291460
